TPU v7x, 128 devices: a whole 4x4x4 slice. The times are simulated.
128 devices in a mesh: seq: 32 (over z, x, y_hi), ffn: 4 (over y_lo, core).
Axes of the slice: x: 4, y: 4 (y_hi: 2, y_lo: 2; y = y_hi * 2 + y_lo), z: 4, core: 2. Of those that a mesh axis runs over, the one named last changes fastest.
Arguments:
- hidden_in: bfloat16 [4, 2048, 2048], P(None, 'seq'), may hold values from -6 to 6
- cotangent: bfloat16 [4, 2048, 2048], P(None, ('seq', 'ffn')), may hold values from -6 to 6
- doc_lengths: int32 [4, 8], replicated, may hold values from 0 to 2048, as said below
- inward: float32 [2048, 3, 2048], P('seq', None, 'ffn'), may hold values from -0.125 to 0.125
- inward_moment: float32 [2048, 3, 2048], P('seq', None, 'ffn'), may hold values from -0.00024414062 to 0.00024414062
- inward_squares: float32 [2048, 3, 2048], P('seq', None, 'ffn'), may hold values from 9.934108e-10 to 3.973643e-09
- outward: float32 [2048, 2048], P('ffn', 'seq'), may hold values from -0.125 to 0.125
- outward_moment: float32 [2048, 2048], P('ffn', 'seq'), may hold values from -0.00024414062 to 0.00024414062
- outward_squares: float32 [2048, 2048], P('ffn', 'seq'), may hold values from 9.934108e-10 to 3.973643e-09
- upward: float32 [2048, 4, 2048], P('seq', None, 'ffn'), may hold values from -0.125 to 0.125
- upward_moment: float32 [2048, 4, 2048], P('seq', None, 'ffn'), may hold values from -0.00024414062 to 0.00024414062
- upward_squares: float32 [2048, 4, 2048], P('seq', None, 'ffn'), may hold values from 9.934108e-10 to 3.973643e-09
- downward: float32 [4, 2048, 2048], P(None, 'ffn', 'seq'), may hold values from -0.0625 to 0.0625
- downward_moment: float32 [4, 2048, 2048], P(None, 'ffn', 'seq'), may hold values from -0.00024414062 to 0.00024414062
- downward_squares: float32 [4, 2048, 2048], P(None, 'ffn', 'seq'), may hold values from 9.934108e-10 to 3.973643e-09
- prenorm: float32 [4, 2048], replicated, may hold values from -0.9 to 2.5
- prenorm_moment: float32 [4, 2048], replicated, may hold values from -0.00024414062 to 0.00024414062
- prenorm_squares: float32 [4, 2048], replicated, may hold values from 9.934108e-10 to 3.973643e-09
- subnorm: float32 [2, 5, 2048], P(None, None, 'ffn'), may hold values from -0.9 to 2.5
- subnorm_moment: float32 [2, 5, 2048], P(None, None, 'ffn'), may hold values from -0.00024414062 to 0.00024414062
- subnorm_squares: float32 [2, 5, 2048], P(None, None, 'ffn'), may hold values from 9.934108e-10 to 3.973643e-09
Outputs:
- hidden_out: bfloat16 [4, 2048, 2048], P(None, ('seq', 'ffn'))
- input_grad: bfloat16 [4, 2048, 2048], P(None, 'seq')
- updated_inward: float32 [2048, 3, 2048], P('seq', None, 'ffn')
- moment_inward: float32 [2048, 3, 2048], P('seq', None, 'ffn')
- squares_inward: float32 [2048, 3, 2048], P('seq', None, 'ffn')
- updated_outward: float32 [2048, 2048], P('ffn', 'seq')
- moment_outward: float32 [2048, 2048], P('ffn', 'seq')
- squares_outward: float32 [2048, 2048], P('ffn', 'seq')
- updated_upward: float32 [2048, 4, 2048], P('seq', None, 'ffn')
- moment_upward: float32 [2048, 4, 2048], P('seq', None, 'ffn')
- squares_upward: float32 [2048, 4, 2048], P('seq', None, 'ffn')
- updated_downward: float32 [4, 2048, 2048], P(None, 'ffn', 'seq')
- moment_downward: float32 [4, 2048, 2048], P(None, 'ffn', 'seq')
- squares_downward: float32 [4, 2048, 2048], P(None, 'ffn', 'seq')
- updated_prenorm: float32 [4, 2048], replicated
- moment_prenorm: float32 [4, 2048], replicated
- squares_prenorm: float32 [4, 2048], replicated
- updated_subnorm: float32 [2, 5, 2048], P(None, None, 'ffn')
- moment_subnorm: float32 [2, 5, 2048], P(None, None, 'ffn')
- squares_subnorm: float32 [2, 5, 2048], P(None, None, 'ffn')
- grad_norm: float32 [], replicated
Inputs may be any that keep to these rules, and one draw needn't show every extreme that they name: `doc_lengths`: each row holds whole documents from its first slot on, in order; a 0 marks an unused entry and all entries after it are 0; every other entry is at least 100; a row's lengths sum to at most 2048, the rest of the row being padding. In each micro-batch of 2 consecutive rows one row is a single document of 2048 tokens.
All inputs are finite; a program needn't handle non-finite values.
Results may differ from a plain program's by a relative error of at most 0.035.
Values may be sent and summed in bfloat16 or wider, within the bound.
No kernel may reach another device: no remote copies, remote signals or barrier semaphores. Data moves between devices by JAX's collectives and lax.ppermute only.
A program may use at most 256 MiB of HBM per device.

v0:
```python
from functools import partial
import functools
import math

import jax
import jax.numpy as jnp
from jax import lax
from jax.sharding import Mesh
from jax.sharding import PartitionSpec as P

HDIM = 64
FF = 8192
MB = 2
STEP = 10
FFN = ("ffn_0", "ffn_1")
SEQ = ("seq_0", "seq_1", "seq_2")
SEQ_FFN = ("seq_0", "seq_1", "seq_2", "ffn_0", "ffn_1")


norm_eps = 1e-05
rope_base = 10000.0
xpos_base = 512.0
clip_limit = 1.0
beta_first = 0.9
beta_second = 0.95
adam_eps = 1e-08
decay_rate = 0.1
matrix_rate = 0.04
norm_rate = 0.6
masked_score = -1e30


def copy_for_each(shard, axis):
    copies = jnp.broadcast_to(shard, (lax.axis_size(axis), *shard.shape))
    return lax.all_to_all(copies, axis, split_axis=0, concat_axis=0, tiled=True)


def of_everyone(shard, axis):
    everything = copy_for_each(shard, axis)
    return jnp.sum(everything, axis=0)


def together(arrays, axis):
    ends = [0]
    for a in arrays:
        ends.append(ends[-1] + a.size)
    subtotal = of_everyone(jnp.concatenate([a.ravel() for a in arrays]), axis)
    return tuple((subtotal[b:e].reshape(a.shape) for a, b, e in zip(arrays, ends, ends[1:])))


def of_everyone_2(shard, axis):
    return copy_for_each(shard, axis).astype(jnp.float32).sum(axis=0)


def gather_turned(arrays, axis, dims):
    turned = [jnp.moveaxis(a, dim, 0) for a, dim in zip(arrays, dims)]
    widths = [t[0].size for t in turned]
    both = jnp.concatenate([t.reshape(-1, w) for t, w in zip(turned, widths)], axis=1)
    filled = lax.all_gather(both, axis, axis=0, tiled=True)
    tiles = jnp.split(filled, [sum(widths[:k]) for k in range(1, len(widths))], axis=1)
    return tuple(
        (
            jnp.moveaxis(b.reshape(-1, *t.shape[1:]), 0, dim)
            for b, t, dim in zip(tiles, turned, dims)
        )
    )


def in_blocks(shard, dim, count):
    shape = shard.shape
    tiles = shard.reshape(*shape[:dim], count, shape[dim] // count, *shape[dim + 1 :])
    return jnp.moveaxis(tiles, dim, 0)


def sent_and_summed(shard, axis, dim):
    count = lax.axis_size(axis)
    tiles = lax.all_to_all(in_blocks(shard, dim, count), axis, 0, 0, tiled=True)
    return jnp.sum(tiles.astype(jnp.float32), axis=0)


def joined_along(tiles, dim):
    tiles = jnp.moveaxis(tiles, 0, dim)
    shape = tiles.shape
    return tiles.reshape(*shape[:dim], shape[dim] * shape[dim + 1], *shape[dim + 2 :])


def gathered_copies(shard, axis, dim):
    tiles = copy_for_each(shard, axis)
    return joined_along(tiles, dim)


def sum_packed(arrays, axis, dims):
    count = lax.axis_size(axis)
    tiles = [in_blocks(a, dim, count) for a, dim in zip(arrays, dims)]
    lines = jnp.concatenate([b.reshape(count, -1) for b in tiles], axis=1)
    width = max(16, -(-lines.shape[1] // 1024) * 8)
    lines = jnp.pad(lines, ((0, 0), (0, width * 128 - lines.shape[1]))).reshape(-1, 128)
    ravelled, at, outs = (lax.psum_scatter(lines, axis, tiled=True).reshape(-1), 0, [])
    for b in tiles:
        part = b[0]
        outs.append(ravelled[at : at + part.size].reshape(part.shape))
        at += part.size
    return tuple(outs)


def over_axes(shard, axes):
    return functools.reduce(lax.psum, axes, shard)


def layout_rows(doc_lengths, row_slots):
    doc_ends = jnp.cumsum(doc_lengths, axis=1)
    places = jnp.arange(row_slots, dtype=jnp.int32)
    segment = jnp.sum((places[None, :, None] >= doc_ends[:, None, :]).astype(jnp.int32), axis=2)
    usable = (places[None, :] < doc_ends[:, -1:]).astype(jnp.float32)
    return (segment, usable)


def xpos_rotate(values, places, direction):
    head_dim = values.shape[-1]
    half_dim = head_dim // 2
    index_half = jnp.arange(half_dim, dtype=jnp.float32)
    inverse = jnp.power(rope_base, -2.0 * index_half / head_dim)
    angles = places[:, None] * inverse[None, :]
    zeta_base = (2.0 * index_half + 0.4 * head_dim) / (1.4 * head_dim)
    stretch = jnp.power(zeta_base[None, :], direction * places[:, None] / xpos_base)
    cosine = (jnp.cos(angles) * stretch)[:, None, :]
    sine_part = (jnp.sin(angles) * stretch)[:, None, :]
    front_half = values[..., :half_dim]
    back_part = values[..., half_dim:]
    return jnp.concatenate(
        [front_half * cosine - back_part * sine_part, front_half * sine_part + back_part * cosine],
        axis=-1,
    )


def plain_norm(values, norm_gain, norm_shift):
    center = jnp.mean(values, axis=-1, keepdims=True)
    spread = jnp.mean(jnp.square(values - center), axis=-1, keepdims=True)
    return (values - center) * lax.rsqrt(spread + norm_eps) * norm_gain + norm_shift


def gelu_exact(values):
    return jax.nn.gelu(values, approximate=False)


def unit_sums(totals, squares):
    return together((totals, squares), FFN)


def head_partials(partial_sum):
    return of_everyone_2(partial_sum.astype(jnp.bfloat16), FFN).astype(jnp.float32)


def split_norm(values, norm_gain, norm_shift, reduce_axes, norm_width):
    totals, squares = unit_sums(
        jnp.sum(values, axis=reduce_axes, keepdims=True),
        jnp.sum(values * values, axis=reduce_axes, keepdims=True),
    )
    center = totals / norm_width
    spread = squares / norm_width - center * center
    inv_spread = lax.rsqrt(spread + norm_eps)
    normed = (values - center) * inv_spread
    return (normed * norm_gain + norm_shift, normed, inv_spread)


def split_norm_back(upstream, norm_gain, normed, inv_spread, reduce_axes, norm_width):
    scaled = upstream * norm_gain
    totals, inner_sum = unit_sums(
        jnp.sum(scaled, axis=reduce_axes, keepdims=True),
        jnp.sum(scaled * normed, axis=reduce_axes, keepdims=True),
    )
    return inv_spread * (scaled - totals / norm_width - normed * inner_sum / norm_width)


def adam_update(weight, moment, squares, gradient, factor, step_rate, decay_weight):
    clipped = gradient * factor
    moment_new = beta_first * moment + (1.0 - beta_first) * clipped
    squares_new = beta_second * squares + (1.0 - beta_second) * clipped * clipped
    moment_hat = moment_new / (1.0 - beta_first**STEP)
    squares_hat = squares_new / (1.0 - beta_second**STEP)
    updated = weight - step_rate * (
        moment_hat / (jnp.sqrt(squares_hat) + adam_eps) + decay_weight * weight
    )
    return (updated, moment_new, squares_new)


def shards(
    hidden_in,
    cotangent,
    doc_lengths,
    inward,
    inward_moment,
    inward_squares,
    outward,
    outward_moment,
    outward_squares,
    upward,
    upward_moment,
    upward_squares,
    downward,
    downward_moment,
    downward_squares,
    prenorm,
    prenorm_moment,
    prenorm_squares,
    subnorm,
    subnorm_moment,
    subnorm_squares,
):
    seq_count = lax.axis_size(SEQ)
    ffn_count = lax.axis_size(FFN)
    seq_index = lax.axis_index(SEQ)
    ffn_index = lax.axis_index(FFN)
    total_rows, local_slots, model_width = hidden_in.shape
    quarter = cotangent.shape[1]
    row_slots = local_slots * seq_count
    batch_rows = total_rows // MB
    local_width = inward.shape[2]
    local_heads = local_width // HDIM
    score_scale = 1.0 / math.sqrt(HDIM)
    segment, usable = layout_rows(doc_lengths, row_slots)
    slot_start = seq_index * local_slots
    local_segment = lax.dynamic_slice_in_dim(segment, slot_start, local_slots, 1)
    local_usable = lax.dynamic_slice_in_dim(usable, slot_start, local_slots, 1)
    all_places = jnp.arange(row_slots, dtype=jnp.int32)
    local_places = slot_start + jnp.arange(local_slots, dtype=jnp.int32)
    offsets = (local_places - row_slots // 2).astype(jnp.float32)
    causal = all_places[None, :] <= local_places[:, None]
    rotate_query = partial(xpos_rotate, places=offsets, direction=1.0)
    rotate_key = partial(xpos_rotate, places=offsets, direction=-1.0)
    shards_low = (
        inward.astype(jnp.bfloat16),
        outward.astype(jnp.bfloat16),
        upward.astype(jnp.bfloat16),
        downward.astype(jnp.bfloat16),
    )
    head_shape = (batch_rows, local_slots, local_heads, HDIM)
    full_shape = (batch_rows, row_slots, local_heads, HDIM)
    pre_grad = jnp.zeros_like(prenorm)
    sub_grad = jnp.zeros_like(subnorm)
    grad_whole = (
        jnp.zeros((model_width, 3, local_width), jnp.float32),
        jnp.zeros((local_width, model_width), jnp.float32),
        jnp.zeros((model_width, 4, local_width), jnp.float32),
        jnp.zeros((4, local_width, model_width), jnp.float32),
    )
    outputs = []
    input_grads = []
    for batch_index in range(MB):
        row_start = batch_index * batch_rows
        row_stop = row_start + batch_rows
        weight_in, weight_mix, weight_up, weight_down = gather_turned(
            (shards_low[0], shards_low[1], shards_low[2], shards_low[3]), SEQ, (0, 1, 0, 2)
        )
        hidden = hidden_in[row_start:row_stop].astype(jnp.float32)
        row_usable = local_usable[row_start:row_stop][..., None]
        allowed = causal[None] & (
            local_segment[row_start:row_stop][:, :, None] == segment[row_start:row_stop][:, None, :]
        )
        normed_one, norm_one_back = jax.vjp(plain_norm, hidden, prenorm[0], prenorm[1])
        input_low = normed_one.astype(jnp.bfloat16)
        project = jnp.einsum(
            "rtd,dke->rtke", input_low, weight_in, preferred_element_type=jnp.float32
        )
        query_rot, query_back = jax.vjp(rotate_query, project[:, :, 0].reshape(head_shape))
        key_rot, key_back = jax.vjp(rotate_key, project[:, :, 1].reshape(head_shape))
        query_low = query_rot.astype(jnp.bfloat16)
        pair_low = jnp.stack(
            [key_rot.reshape(batch_rows, local_slots, local_width), project[:, :, 2]], axis=2
        ).astype(jnp.bfloat16)
        all_pairs = lax.all_gather(pair_low, SEQ, axis=1, tiled=True)
        key_all = all_pairs[:, :, 0].reshape(full_shape)
        value_all = all_pairs[:, :, 1].reshape(full_shape)
        scores = (
            jnp.einsum("rqhe,rkhe->rhqk", query_low, key_all, preferred_element_type=jnp.float32)
            * score_scale
        )
        scores = jnp.where(allowed[:, None], scores, masked_score)
        peak_score = jnp.max(scores, axis=-1, keepdims=True)
        exponent = jnp.exp(scores - peak_score)
        row_total = jnp.sum(exponent, axis=-1, keepdims=True)
        log_total = peak_score + jnp.log(row_total)
        chances_low = (exponent / row_total).astype(jnp.bfloat16)
        attended = jnp.einsum(
            "rhqk,rkhe->rqhe", chances_low, value_all, preferred_element_type=jnp.float32
        ).reshape(batch_rows, local_slots, local_width)
        mixed_norm, mixed_hat, mixed_inv = split_norm(
            attended, subnorm[0, 0], subnorm[1, 0], (2,), model_width
        )
        mixed_low = mixed_norm.astype(jnp.bfloat16)
        branch = head_partials(
            jnp.einsum("rtc,cd->rtd", mixed_low, weight_mix, preferred_element_type=jnp.float32)
        )
        first_sum = hidden + row_usable * branch
        normed_three, norm_three_back = jax.vjp(plain_norm, first_sum, prenorm[2], prenorm[3])
        middle_low = normed_three.astype(jnp.bfloat16)
        upper_proj = jnp.einsum(
            "rtd,dbc->rtbc", middle_low, weight_up, preferred_element_type=jnp.float32
        )
        activated, gelu_back = jax.vjp(gelu_exact, upper_proj)
        inner_norm, inner_hat, inner_inv = split_norm(
            activated, subnorm[0, 1:], subnorm[1, 1:], (2, 3), FF
        )
        inner_low = inner_norm.astype(jnp.bfloat16)
        lowered = jnp.einsum(
            "rtbc,bcd->rtd", inner_low, weight_down, preferred_element_type=jnp.float32
        )
        reduced = sent_and_summed(lowered.astype(jnp.bfloat16), FFN, 1)
        own_start = ffn_index * quarter
        residual_part = lax.dynamic_slice_in_dim(first_sum, own_start, quarter, 1)
        usable_part = lax.dynamic_slice_in_dim(row_usable, own_start, quarter, 1)
        outputs.append((residual_part + usable_part * reduced).astype(jnp.bfloat16))
        cot_full = gathered_copies(cotangent[row_start:row_stop], FFN, 1).astype(jnp.float32)
        cot_low = (row_usable * cot_full).astype(jnp.bfloat16)
        grad_down = jnp.einsum(
            "rtbc,rtd->bcd", inner_low, cot_low, preferred_element_type=jnp.float32
        )
        back_inner = jnp.einsum(
            "rtd,bcd->rtbc", cot_low, weight_down, preferred_element_type=jnp.float32
        )
        inner_gain_grad = jnp.sum(back_inner * inner_hat, axis=(0, 1))
        inner_shift_grad = jnp.sum(back_inner, axis=(0, 1))
        back_act = split_norm_back(back_inner, subnorm[0, 1:], inner_hat, inner_inv, (2, 3), FF)
        upper_low = gelu_back(back_act)[0].astype(jnp.bfloat16)
        grad_up = jnp.einsum(
            "rtd,rtbc->dbc", middle_low, upper_low, preferred_element_type=jnp.float32
        )
        back_middle = head_partials(
            jnp.einsum("rtbc,dbc->rtd", upper_low, weight_up, preferred_element_type=jnp.float32)
        )
        back_first_norm, gain_three_grad, shift_three_grad = norm_three_back(back_middle)
        back_first = cot_full + back_first_norm
        branch_low = (row_usable * back_first).astype(jnp.bfloat16)
        grad_mix = jnp.einsum(
            "rtc,rtd->cd", mixed_low, branch_low, preferred_element_type=jnp.float32
        )
        back_mixed = jnp.einsum(
            "rtd,cd->rtc", branch_low, weight_mix, preferred_element_type=jnp.float32
        )
        mixed_gain_grad = jnp.sum(back_mixed * mixed_hat, axis=(0, 1))
        mixed_shift_grad = jnp.sum(back_mixed, axis=(0, 1))
        back_attended = split_norm_back(
            back_mixed, subnorm[0, 0], mixed_hat, mixed_inv, (2,), model_width
        )
        attend_low = back_attended.astype(jnp.bfloat16).reshape(head_shape)
        scores = (
            jnp.einsum("rqhe,rkhe->rhqk", query_low, key_all, preferred_element_type=jnp.float32)
            * score_scale
        )
        scores = jnp.where(allowed[:, None], scores, masked_score)
        chances = jnp.exp(scores - log_total)
        back_chances = jnp.einsum(
            "rqhe,rkhe->rhqk", attend_low, value_all, preferred_element_type=jnp.float32
        )
        inner_sum = jnp.sum(chances * back_chances, axis=-1, keepdims=True)
        score_low = (chances * (back_chances - inner_sum)).astype(jnp.bfloat16)
        back_query = (
            jnp.einsum("rhqk,rkhe->rqhe", score_low, key_all, preferred_element_type=jnp.float32)
            * score_scale
        )
        back_key = (
            jnp.einsum("rhqk,rqhe->rkhe", score_low, query_low, preferred_element_type=jnp.float32)
            * score_scale
        )
        back_value = jnp.einsum(
            "rhqk,rqhe->rkhe",
            chances.astype(jnp.bfloat16),
            attend_low,
            preferred_element_type=jnp.float32,
        )
        back_pairs = jnp.stack(
            [
                back_key.reshape(batch_rows, row_slots, local_width),
                back_value.reshape(batch_rows, row_slots, local_width),
            ],
            axis=2,
        )
        own_pairs = lax.psum_scatter(
            back_pairs.astype(jnp.bfloat16), SEQ, scatter_dimension=1, tiled=True
        ).astype(jnp.float32)
        query_grad = query_back(back_query)[0].reshape(batch_rows, local_slots, local_width)
        key_grad = key_back(own_pairs[:, :, 0].reshape(head_shape))[0].reshape(
            batch_rows, local_slots, local_width
        )
        project_low = jnp.stack([query_grad, key_grad, own_pairs[:, :, 1]], axis=2).astype(
            jnp.bfloat16
        )
        grad_in = jnp.einsum(
            "rtd,rtke->dke", input_low, project_low, preferred_element_type=jnp.float32
        )
        back_input = head_partials(
            jnp.einsum("rtke,dke->rtd", project_low, weight_in, preferred_element_type=jnp.float32)
        )
        back_hidden, gain_one_grad, shift_one_grad = norm_one_back(back_input)
        input_grads.append((back_first + back_hidden).astype(jnp.bfloat16))
        pre_grad = pre_grad + jnp.stack(
            [gain_one_grad, shift_one_grad, gain_three_grad, shift_three_grad]
        )
        sub_grad = sub_grad + jnp.stack(
            [
                jnp.concatenate([mixed_gain_grad[None], inner_gain_grad], axis=0),
                jnp.concatenate([mixed_shift_grad[None], inner_shift_grad], axis=0),
            ]
        )
        local_grads = (grad_in, grad_mix, grad_up, grad_down)
        grad_whole = jax.tree.map(jnp.add, grad_whole, local_grads)
    grad_shards = tuple(
        (
            part.astype(jnp.float32)
            for part in sum_packed(
                (
                    grad_whole[0].astype(jnp.bfloat16),
                    grad_whole[1].astype(jnp.bfloat16),
                    grad_whole[2].astype(jnp.bfloat16),
                    grad_whole[3].astype(jnp.bfloat16),
                ),
                SEQ,
                (0, 1, 0, 2),
            )
        )
    )
    pre_total, sub_total = (
        of_everyone_2(pre_grad.astype(jnp.bfloat16), SEQ).astype(jnp.float32),
        of_everyone_2(sub_grad.astype(jnp.bfloat16), SEQ).astype(jnp.float32),
    )
    local_squares = sum((jnp.sum(shard_grad * shard_grad) for shard_grad in grad_shards))
    local_squares = (
        local_squares
        + jnp.sum(sub_total * sub_total) / seq_count
        + jnp.sum(pre_total * pre_total) / (seq_count * ffn_count)
    )
    total_squares = over_axes(local_squares, SEQ_FFN)
    grad_norm = jnp.sqrt(total_squares)
    factor = jnp.minimum(1.0, clip_limit / (grad_norm + 1e-06))
    updated_inward, moment_inward, squares_inward = adam_update(
        inward, inward_moment, inward_squares, grad_shards[0], factor, matrix_rate, decay_rate
    )
    updated_outward, moment_outward, squares_outward = adam_update(
        outward, outward_moment, outward_squares, grad_shards[1], factor, matrix_rate, decay_rate
    )
    updated_upward, moment_upward, squares_upward = adam_update(
        upward, upward_moment, upward_squares, grad_shards[2], factor, matrix_rate, decay_rate
    )
    updated_downward, moment_downward, squares_downward = adam_update(
        downward, downward_moment, downward_squares, grad_shards[3], factor, matrix_rate, decay_rate
    )
    updated_prenorm, moment_prenorm, squares_prenorm = adam_update(
        prenorm, prenorm_moment, prenorm_squares, pre_total, factor, norm_rate, 0.0
    )
    updated_subnorm, moment_subnorm, squares_subnorm = adam_update(
        subnorm, subnorm_moment, subnorm_squares, sub_total, factor, norm_rate, 0.0
    )
    hidden_out = jnp.concatenate(outputs, axis=0)
    input_grad = jnp.concatenate(input_grads, axis=0)
    return (
        hidden_out,
        input_grad,
        updated_inward,
        moment_inward,
        squares_inward,
        updated_outward,
        moment_outward,
        squares_outward,
        updated_upward,
        moment_upward,
        squares_upward,
        updated_downward,
        moment_downward,
        squares_downward,
        updated_prenorm,
        moment_prenorm,
        squares_prenorm,
        updated_subnorm,
        moment_subnorm,
        squares_subnorm,
        grad_norm,
    )


def solution(mesh):
    finer = Mesh(mesh.devices.reshape(4, 4, 2, 2, 2), ("seq_0", "seq_1", "seq_2", "ffn_0", "ffn_1"))
    placed = (
        P(None, SEQ, None),
        P(None, SEQ_FFN, None),
        P(),
        P(SEQ, None, FFN),
        P(SEQ, None, FFN),
        P(SEQ, None, FFN),
        P(FFN, SEQ),
        P(FFN, SEQ),
        P(FFN, SEQ),
        P(SEQ, None, FFN),
        P(SEQ, None, FFN),
        P(SEQ, None, FFN),
        P(None, FFN, SEQ),
        P(None, FFN, SEQ),
        P(None, FFN, SEQ),
        P(),
        P(),
        P(),
        P(None, None, FFN),
        P(None, None, FFN),
        P(None, None, FFN),
    )
    return jax.shard_map(
        shards,
        mesh=finer,
        in_specs=placed,
        out_specs=(
            P(None, SEQ_FFN, None),
            P(None, SEQ, None),
            P(SEQ, None, FFN),
            P(SEQ, None, FFN),
            P(SEQ, None, FFN),
            P(FFN, SEQ),
            P(FFN, SEQ),
            P(FFN, SEQ),
            P(SEQ, None, FFN),
            P(SEQ, None, FFN),
            P(SEQ, None, FFN),
            P(None, FFN, SEQ),
            P(None, FFN, SEQ),
            P(None, FFN, SEQ),
            P(),
            P(),
            P(),
            P(None, None, FFN),
            P(None, None, FFN),
            P(None, None, FFN),
            P(),
        ),
        check_vma=False,
    )
```

profile of v0, /device:TPU:1, one launch (start us, length us, event | category | flops | bytes accessed | tf_op | source)
XLA Modules:
  0.0 1752.9 jit_solution(7627228856568584737)
XLA Ops:
  17.8 204.9 %all-gather.4.cloned.1.call-done = bf16[2048,6144]{1,0:T(8,128)(2,1)} async-done(((bf16[64,6144]{1,0:T(8,128)(2,1)}), bf16[2048,6144]{1,0:T(8,128)(2,1)}) %all-gather.4.cloned.1.call-update) | async-done | bytes 25165840 | tf_op jit(solution)/shard_map/all_gather | solution.py:59
  228.6 8.8 copy.451
  260.4 93.3 %all-gather.6.cloned.1.call-done = bf16[2,2048,2,512]{3,1,2,0:T(8,128)(2,1)} async-done(((bf16[2,64,2,512]{3,1,2,0:T(8,128)(2,1)}), bf16[2,2048,2,512]{3,1,2,0:T(8,128)(2,1)}) %all-gather.6.cloned.1.call-update) | async-done | bytes 8388624 | tf_op jit(solution)/shard_map/all_gather | solution.py:271
  365.7 6.3 copy.456
  385.5 73.7 %all-gather.8.cloned.1.call-done = bf16[2,2048,2,512]{3,1,2,0:T(8,128)(2,1)} async-done(((bf16[2,64,2,512]{3,1,2,0:T(8,128)(2,1)}), bf16[2,2048,2,512]{3,1,2,0:T(8,128)(2,1)}) %all-gather.8.cloned.1.call-update) | async-done | bytes 8388624 | tf_op jit(solution)/shard_map/all_gather | solution.py:271
  492.0 7.8 all-to-all-done.13
  519.4 20.4 %all-to-all-done.1 = bf16[4,2,64,2048]{3,2,1,0:T(8,128)(2,1)} async-done(((bf16[4,2,64,2048]{3,2,1,0:T(8,128)(2,1)}), bf16[4,2,64,2048]{3,2,1,0:T(8,128)(2,1)}, u32[]{:S(2)}, u32[]{:S(2)}) %all-to-all-start.1) | async-done | bytes 2097184 | tf_op jit(solution)/shard_map/all_to_all | solution.py:35
  547.2 11.9 fusion.161
  559.1 12.3 copy.544
  613.8 7.6 fusion.97
  628.6 8.6 multiply_reduce_fusion.5
  659.1 6.3 fusion.33
  672.1 7.3 fusion.32
  679.4 17.6 %all-to-all-done.10 = bf16[4,2,64,2048]{3,2,1,0:T(8,128)(2,1)} async-done(((bf16[4,2,64,2048]{3,2,1,0:T(8,128)(2,1)}), bf16[4,2,64,2048]{3,2,1,0:T(8,128)(2,1)}, u32[]{:S(2)}, u32[]{:S(2)}) %all-to-all-start.10) | async-done | bytes 2097184 | tf_op jit(solution)/shard_map/all_to_all | solution.py:35
  709.1 20.9 %all-to-all-done.15 = bf16[4,2,64,2048]{3,2,1,0:T(8,128)(2,1)} async-done(((bf16[4,2,64,2048]{3,2,1,0:T(8,128)(2,1)}), bf16[4,2,64,2048]{3,2,1,0:T(8,128)(2,1)}, u32[]{:S(2)}, u32[]{:S(2)}) %all-to-all-start.15) | async-done | bytes 2097184 | tf_op jit(solution)/shard_map/all_to_all | solution.py:35
  765.4 6.8 fusion.24
  772.2 7.1 multiply_reduce_fusion.1
  785.6 6.8 multiply_convert_fusion.3
  804.1 7.5 pad_maximum_fusion.1
  813.1 6.7 fusion.27
  826.0 7.0 multiply_reduce_fusion
  849.0 7.5 pad_maximum_fusion.2
  857.3 9.3 fusion.99
  866.6 11.5 fusion.1
  878.1 11.8 copy.507
  889.9 15.7 copy.508
  905.6 16.1 reshape.924
  921.7 9.3 fusion.146
  931.0 11.5 fusion
  942.6 12.2 copy.506
  954.8 10.3 reshape_reshape.7
  999.4 201.2 %reduce-scatter.6.cloned.1.call-done = bf16[2,64,2,512]{3,1,2,0:T(8,128)(2,1)} async-done(((bf16[2,2048,2,512]{3,1,2,0:T(8,128)(2,1)}), bf16[2,64,2,512]{3,1,2,0:T(8,128)(2,1)}) %reduce-scatter.6.cloned.1.call-update) | async-done | bytes 262160 | tf_op jit(solution)/shard_map/reduce_scatter | solution.py:378
  1214.6 27.6 %copy.501 = bf16[2048,3,512]{2,1,0:T(4,128)(2,1)} copy(bf16[2048,3,512]{2,0,1:T(8,128)(2,1)S(1)} %fusion.2) | data formatting | bytes 12582912 | tf_op jit(solution)/shard_map/convert_element_type | solution.py:412
  1242.2 11.2 reshape_reshape.6
  1253.4 37.4 %pad_maximum_fusion = bf16[32,393216]{1,0:T(8,128)(2,1)} fusion(bf16[32,131072]{1,0:T(8,128)(2,1)} %reshape.924, bf16[32,131072]{1,0:T(8,128)(2,1)} %reshape_reshape.7, bf16[32,32768]{1,0:T(8,128)(2,1)} %reshape.922, bf16[32,98304]{1,0:T(8,128)(2,1)} %reshape_reshape.6), kind=kLoop, calls=%fused_computation | loop fusion | flops 100663296 | bytes 50331648 | tf_op jit(solution)/shard_map/concatenate | solution.py:95
  1290.9 33.4 %reshape.925 = bf16[98304,128]{1,0:T(8,128)(2,1)} reshape(bf16[32,393216]{1,0:T(8,128)(2,1)} %pad_maximum_fusion) | data formatting | bytes 50331648 | tf_op jit(solution)/shard_map/reshape | solution.py:97
  1330.6 22.2 %all-to-all-start.7 = ((bf16[4,2,16,2048]{3,2,1,0:T(8,128)(2,1)}), bf16[4,2,16,2048]{3,2,1,0:T(8,128)(2,1)S(1)}, u32[]{:S(2)}, u32[]{:S(2)}) async-start(bf16[4,2,16,2048]{3,2,1,0:T(8,128)(2,1)} %bitcast.340), calls=%async_computation.7 | async-start | bytes 1048576 | tf_op jit(solution)/shard_map/all_to_all | solution.py:77
  1367.5 12.2 all-to-all-done.3
  1380.6 10.1 all-to-all-start.18
  1395.0 8.6 all-to-all-done.18
  1405.1 7.4 all-to-all-start.12
  1417.6 27.5 %all-to-all-done.12 = bf16[4,2,64,2048]{3,2,1,0:T(8,128)(2,1)} async-done(((bf16[4,2,64,2048]{3,2,1,0:T(8,128)(2,1)}), bf16[4,2,64,2048]{3,2,1,0:T(8,128)(2,1)}, u32[]{:S(2)}, u32[]{:S(2)}) %all-to-all-start.12) | async-done | bytes 2097184 | tf_op jit(solution)/shard_map/all_to_all | solution.py:35
  1459.8 28.6 %all-to-all-done.17 = bf16[4,2,64,2048]{3,2,1,0:T(8,128)(2,1)} async-done(((bf16[4,2,64,2048]{3,2,1,0:T(8,128)(2,1)}), bf16[4,2,64,2048]{3,2,1,0:T(8,128)(2,1)}, u32[]{:S(2)}, u32[]{:S(2)}) %all-to-all-start.17) | async-done | bytes 2097184 | tf_op jit(solution)/shard_map/all_to_all | solution.py:35
  1501.9 10.0 all-to-all-done.19
  1514.6 158.3 %reduce-scatter.8.cloned.1.call-done = bf16[3072,128]{1,0:T(8,128)(2,1)} async-done(((bf16[98304,128]{1,0:T(8,128)(2,1)}), bf16[3072,128]{1,0:T(8,128)(2,1)}) %reduce-scatter.8.cloned.1.call-update) | async-done | bytes 786448 | tf_op jit(solution)/shard_map/reduce_scatter | solution.py:98
  1680.8 8.1 psum.35
  1689.5 7.8 psum.36
  1714.0 11.4 psum.39
  (595 shorter events, 443.0 us)
Async XLA Ops:
  7.2 215.5 %all-gather.4.cloned.1.call-start = ((), (), s32[]{:S(2)}) async-start(), calls=%async_computation.23 | async-start | bytes 25952256 | tf_op jit(solution)/shard_map/all_gather | solution.py:59
  12.5 341.2 %all-gather.6.cloned.1.call-start = ((), (), s32[]{:S(2)}) async-start(), calls=%async_computation.24 | async-start | bytes 8650752 | tf_op jit(solution)/shard_map/all_gather | solution.py:271
  14.5 222.9 %copy-start.86 = (f32[2,64]{1,0:T(2,128)}, f32[2,64]{1,0:T(2,128)S(1)}, u32[]{:S(2)}) copy-start(f32[2,64]{1,0:T(2,128)S(1)} %get-tuple-element.339) | copy-start | bytes 1540
  14.5 228.9 %copy-start.83 = (f32[2,64]{1,0:T(2,128)}, f32[2,64]{1,0:T(2,128)S(1)}, u32[]{:S(2)}) copy-start(f32[2,64]{1,0:T(2,128)S(1)} %get-tuple-element.338) | copy-start | bytes 1540
  16.1 221.3 %copy-start.134 = (f32[2,64]{1,0:T(2,128)}, f32[2,64]{1,0:T(2,128)S(1)}, u32[]{:S(2)}) copy-start(f32[2,64]{1,0:T(2,128)S(1)} %get-tuple-element.165) | copy-start | bytes 1540
  16.2 221.3 %copy-start.135 = (f32[2,64]{1,0:T(2,128)}, f32[2,64]{1,0:T(2,128)S(1)}, u32[]{:S(2)}) copy-start(f32[2,64]{1,0:T(2,128)S(1)} %get-tuple-element.164) | copy-start | bytes 1540
  16.2 221.3 %copy-start.109 = (f32[2,64]{1,0:T(2,128)}, f32[2,64]{1,0:T(2,128)S(1)}, u32[]{:S(2)}) copy-start(f32[2,64]{1,0:T(2,128)S(1)} %fusion.132) | copy-start | bytes 1540
  16.2 227.2 %copy-start.111 = (f32[2,64]{1,0:T(2,128)}, f32[2,64]{1,0:T(2,128)S(1)}, u32[]{:S(2)}) copy-start(f32[2,64]{1,0:T(2,128)S(1)} %fusion.134) | copy-start | bytes 1540
  17.8 225.6 %copy-start.50 = (f32[1,2048]{1,0:T(1,128)}, f32[1,2048]{1,0:T(1,128)S(1)}, u32[]{:S(2)}) copy-start(f32[1,2048]{1,0:T(1,128)S(1)} %get-tuple-element.269) | copy-start | bytes 24580
  17.8 225.6 %copy-start.56 = (f32[1,2048]{1,0:T(1,128)}, f32[1,2048]{1,0:T(1,128)S(1)}, u32[]{:S(2)}) copy-start(f32[1,2048]{1,0:T(1,128)S(1)} %get-tuple-element.268) | copy-start | bytes 24580
  251.7 207.6 %all-gather.8.cloned.1.call-start = ((), (), s32[]{:S(2)}) async-start(), calls=%async_computation.25 | async-start | bytes 8650752 | tf_op jit(solution)/shard_map/all_gather | solution.py:271
  254.9 262.0 %copy-start.95 = (f32[1,1,512]{2,0,1:T(1,128)}, f32[1,1,512]{2,0,1:T(1,128)S(1)}, u32[]{:S(2)}) copy-start(f32[1,1,512]{2,0,1:T(1,128)S(1)} %get-tuple-element.273) | copy-start | bytes 6148
  260.3 217.4 %copy-start.29 = (bf16[2,64,8,32]{3,1,2,0:T(8,128)(2,1)}, bf16[2,64,8,32]{3,1,2,0:T(8,128)(2,1)S(1)}, u32[]{:S(2)}) copy-start(bf16[2,64,8,32]{3,1,2,0:T(8,128)(2,1)S(1)} %get-tuple-element.261) | copy-start | bytes 196612
  260.4 217.4 %copy-start.31 = (bf16[2,64,8,32]{3,1,2,0:T(8,128)(2,1)}, bf16[2,64,8,32]{3,1,2,0:T(8,128)(2,1)S(1)}, u32[]{:S(2)}) copy-start(bf16[2,64,8,32]{3,1,2,0:T(8,128)(2,1)S(1)} %get-tuple-element.262) | copy-start | bytes 196612
  381.2 105.2 %all-to-all-start = ((f32[4,1,256]{2,1,0:T(1,128)}), f32[4,1,256]{2,1,0:T(1,128)S(1)}, u32[]{:S(2)}, u32[]{:S(2)}) async-start(f32[4,1,256]{2,1,0:T(1,128)} %broadcast_in_dim.80), calls=%async_computation | async-start | bytes 8192 | tf_op jit(solution)/shard_map/all_to_all | solution.py:35
  486.4 275.9 %copy-start.33 = (f32[2,64,512]{2,1,0:T(8,128)}, f32[2,64,512]{2,1,0:T(8,128)S(1)}, u32[]{:S(2)}) copy-start(f32[2,64,512]{2,1,0:T(8,128)S(1)} %copy.458) | copy-start | bytes 786436
  487.3 12.5 all-to-all-start.13
  500.4 7.7 all-to-all-start.4
  509.8 30.0 %all-to-all-start.1 = ((bf16[4,2,64,2048]{3,2,1,0:T(8,128)(2,1)}), bf16[4,2,64,2048]{3,2,1,0:T(8,128)(2,1)}, u32[]{:S(2)}, u32[]{:S(2)}) async-start(bf16[4,2,64,2048]{3,2,1,0:T(8,128)(2,1)} %broadcast_in_dim.81), calls=%async_computation.1 | async-start | bytes 4194304 | tf_op jit(solution)/shard_map/all_to_all | solution.py:35
  541.4 30.2 %all-to-all-start.5 = ((bf16[4,2,64,2048]{3,2,1,0:T(8,128)(2,1)}), bf16[4,2,64,2048]{3,2,1,0:T(8,128)(2,1)}, u32[]{:S(2)}, u32[]{:S(2)}) async-start(bf16[4,2,64,2048]{3,2,1,0:T(8,128)(2,1)} %broadcast_in_dim.85), calls=%async_computation.5 | async-start | bytes 4194304 | tf_op jit(solution)/shard_map/all_to_all | solution.py:35
  572.5 12.3 all-to-all-start.8
  588.2 149.9 %copy-start.77 = (f32[2,64]{1,0:T(2,128)}, f32[2,64]{1,0:T(2,128)S(1)}, u32[]{:S(2)}) copy-start(f32[2,64]{1,0:T(2,128)S(1)} %broadcast_multiply_fusion) | copy-start | bytes 1540
  588.4 149.6 %copy-start.88 = (f32[2,64]{1,0:T(2,128)}, f32[2,64]{1,0:T(2,128)S(1)}, u32[]{:S(2)}) copy-start(f32[2,64]{1,0:T(2,128)S(1)} %fusion.135) | copy-start | bytes 1540
  599.2 22.2 %all-to-all-start.6 = ((f32[4,1,256]{2,1,0:T(1,128)}), f32[4,1,256]{2,1,0:T(1,128)S(1)}, u32[]{:S(2)}, u32[]{:S(2)}) async-start(f32[4,1,256]{2,1,0:T(1,128)} %broadcast_in_dim.86), calls=%async_computation.6 | async-start | bytes 8192 | tf_op jit(solution)/shard_map/all_to_all | solution.py:35
  613.6 243.6 %copy-start.8 = (f32[2,64,4,512]{3,1,2,0:T(8,128)}, f32[2,64,4,512]{3,1,2,0:T(8,128)S(1)}, u32[]{:S(2)}) copy-start(f32[2,64,4,512]{3,1,2,0:T(8,128)S(1)} %get-tuple-element.205) | copy-start | bytes 3145732
  622.0 6.4 all-to-all-start.2
  638.0 7.0 all-to-all-start.9
  645.6 7.4 all-to-all-start.14
  667.0 30.1 %all-to-all-start.10 = ((bf16[4,2,64,2048]{3,2,1,0:T(8,128)(2,1)}), bf16[4,2,64,2048]{3,2,1,0:T(8,128)(2,1)}, u32[]{:S(2)}, u32[]{:S(2)}) async-start(bf16[4,2,64,2048]{3,2,1,0:T(8,128)(2,1)} %broadcast_in_dim.89), calls=%async_computation.10 | async-start | bytes 4194304 | tf_op jit(solution)/shard_map/all_to_all | solution.py:35
  699.7 30.2 %all-to-all-start.15 = ((bf16[4,2,64,2048]{3,2,1,0:T(8,128)(2,1)}), bf16[4,2,64,2048]{3,2,1,0:T(8,128)(2,1)}, u32[]{:S(2)}, u32[]{:S(2)}) async-start(bf16[4,2,64,2048]{3,2,1,0:T(8,128)(2,1)} %broadcast_in_dim.96), calls=%async_computation.16 | async-start | bytes 4194304 | tf_op jit(solution)/shard_map/all_to_all | solution.py:35
  746.2 7.2 all-to-all-start.11
  754.0 7.0 all-to-all-start.16
  757.9 238.9 %reduce-scatter.4.cloned.1.call-start = ((), (), s32[]{:S(2)}) async-start(), calls=%async_computation.26 | async-start | bytes 8650752 | tf_op jit(solution)/shard_map/reduce_scatter | solution.py:378
  811.6 389.0 %reduce-scatter.6.cloned.1.call-start = ((), (), s32[]{:S(2)}) async-start(), calls=%async_computation.27 | async-start | bytes 8650752 | tf_op jit(solution)/shard_map/reduce_scatter | solution.py:378
  856.5 816.4 %reduce-scatter.8.cloned.1.call-start = ((), (), s32[]{:S(2)}) async-start(), calls=%async_computation.28 | async-start | bytes 25952256 | tf_op jit(solution)/shard_map/reduce_scatter | solution.py:98
  993.7 215.8 %copy-start.3 = (bf16[4,64,2048]{2,1,0:T(8,128)(2,1)S(1)}, bf16[4,64,2048]{2,1,0:T(8,128)(2,1)}, u32[]{:S(2)}) copy-start(bf16[4,64,2048]{2,1,0:T(8,128)(2,1)} %param.21) | copy-start | bytes 3145732
  996.8 215.8 %copy-start.46 = (bf16[2,64,1,512]{3,1,0,2:T(8,128)(2,1)}, bf16[2,64,1,512]{3,1,0,2:T(8,128)(2,1)S(1)}, u32[]{:S(2)}) copy-start(bf16[2,64,1,512]{3,1,0,2:T(8,128)(2,1)S(1)} %stack_reshape.46) | copy-start | bytes 393220
  1330.6 32.8 %all-to-all-start.7 = ((bf16[4,2,16,2048]{3,2,1,0:T(8,128)(2,1)}), bf16[4,2,16,2048]{3,2,1,0:T(8,128)(2,1)S(1)}, u32[]{:S(2)}, u32[]{:S(2)}) async-start(bf16[4,2,16,2048]{3,2,1,0:T(8,128)(2,1)} %bitcast.340), calls=%async_computation.7 | async-start | bytes 1048576 | tf_op jit(solution)/shard_map/all_to_all | solution.py:77
  1363.3 16.3 all-to-all-start.3
  1380.6 23.0 %all-to-all-start.18 = ((bf16[32,2,5,512]{3,1,2,0:T(2,128)(2,1)}), bf16[32,2,5,512]{3,1,2,0:T(2,128)(2,1)S(1)}, u32[]{:S(2)}, u32[]{:S(2)}) async-start(bf16[32,2,5,512]{3,1,2,0:T(2,128)(2,1)} %broadcast_in_dim.198), calls=%async_computation.21 | async-start | bytes 655360 | tf_op jit(solution)/shard_map/all_to_all | solution.py:35
  1405.1 40.0 %all-to-all-start.12 = ((bf16[4,2,64,2048]{3,2,1,0:T(8,128)(2,1)}), bf16[4,2,64,2048]{3,2,1,0:T(8,128)(2,1)}, u32[]{:S(2)}, u32[]{:S(2)}) async-start(bf16[4,2,64,2048]{3,2,1,0:T(8,128)(2,1)} %broadcast_in_dim.92), calls=%async_computation.13 | async-start | bytes 4194304 | tf_op jit(solution)/shard_map/all_to_all | solution.py:35
  1446.8 41.6 %all-to-all-start.17 = ((bf16[4,2,64,2048]{3,2,1,0:T(8,128)(2,1)}), bf16[4,2,64,2048]{3,2,1,0:T(8,128)(2,1)}, u32[]{:S(2)}, u32[]{:S(2)}) async-start(bf16[4,2,64,2048]{3,2,1,0:T(8,128)(2,1)} %broadcast_in_dim.99), calls=%async_computation.19 | async-start | bytes 4194304 | tf_op jit(solution)/shard_map/all_to_all | solution.py:35
  1452.9 251.1 %copy-start.14 = (f32[2,64,2048]{2,1,0:T(8,128)S(1)}, f32[2,64,2048]{2,1,0:T(8,128)}, u32[]{:S(2)}) copy-start(f32[2,64,2048]{2,1,0:T(8,128)} %copy-done.12) | copy-start | bytes 3145732
  1457.3 240.6 %copy-start.60 = (f32[2,5,512]{2,0,1:T(2,128)}, f32[2,5,512]{2,0,1:T(2,128)S(1)}, u32[]{:S(2)}) copy-start(f32[2,5,512]{2,0,1:T(2,128)S(1)} %convert_reduce_fusion.15) | copy-start | bytes 61444
  1494.7 17.2 all-to-all-start.19
  1501.3 196.6 %copy-start.132 = (f32[2,64]{1,0:T(2,128)}, f32[2,64]{1,0:T(2,128)S(1)}, u32[]{:S(2)}) copy-start(f32[2,64]{1,0:T(2,128)S(1)} %multiply_multiply_fusion.20) | copy-start | bytes 1540
  1501.9 196.0 %copy-start.133 = (f32[2,64]{1,0:T(2,128)}, f32[2,64]{1,0:T(2,128)S(1)}, u32[]{:S(2)}) copy-start(f32[2,64]{1,0:T(2,128)S(1)} %multiply_multiply_fusion.18) | copy-start | bytes 1540
  1513.3 184.6 %copy-start.55 = (f32[4,2048]{1,0:T(4,128)}, f32[4,2048]{1,0:T(4,128)S(1)}, u32[]{:S(2)}) copy-start(f32[4,2048]{1,0:T(4,128)S(1)} %convert_reduce_fusion.12) | copy-start | bytes 98308
  (122 other events, 2620.1 us)
Sparse Core Ops, SparseCore 0:
  12.6 210.0 all-gather.3
  251.8 101.8 all-gather.5
  357.3 101.8 all-gather.7
  811.7 183.4 reduce-scatter.3
  997.5 203.0 reduce-scatter.5
  1324.4 348.4 reduce-scatter.7
where the time goes:
time: 1760 us; the launch traced here: 1750 us
  waiting for transfers between devices  906 us (51%)
  local copies, waits for them, and re-layouts  311 us (18%)
  matrix products  185 us (11%)
  other arithmetic  174 us (10%)
  starting transfers between devices  117 us (7%)
  blocking collectives  37.9 us (2%)
  between operations  22 us (1%)
    all_gather x1, waiting for transfers between devices, gather_turned(): filled = lax.all_gather(both, axis, axis=0, tiled=True)  205 us
    reduce_scatter x2, waiting for transfers between devices, shards(): lax.psum_scatter(back_pairs.astype(jnp.bfloat16), SEQ, scatter_dimension=...  201 us
    all_gather x2, waiting for transfers between devices, shards(): all_pairs = lax.all_gather(pair_low, SEQ, axis=1, tiled=True)  167 us
    reduce_scatter x1, waiting for transfers between devices, sum_packed(): lax.psum_scatter(lines, axis, tiled=True).reshape(-1)  158 us
    all_to_all x18, waiting for transfers between devices, copy_for_each(): return lax.all_to_all(copies, axis, split_axis=0, concat_axis=0, tiled=True)  157 us
    all_to_all x18, starting transfers between devices, copy_for_each(): return lax.all_to_all(copies, axis, split_axis=0, concat_axis=0, tiled=True)  90.6 us
    psum x5, blocking collectives, over_axes(): return functools.reduce(lax.psum, axes, shard)  37.9 us
    concatenate x1, other arithmetic, sum_packed(): lines = jnp.concatenate([b.reshape(count, -1) for b in tiles], axis=1)  37.4 us
  transfers between devices with their start and end apart: 26, of which 23 were waited for; matrix products, arithmetic and copies ran while one was open for 21% of the time, Pallas kernels for 0%

commit v1 on v0

v1 whole, which is shorter than its diff:
```python
import functools
import math

import jax
import jax.numpy as jnp
import numpy as np
from jax import lax
from jax.experimental import pallas as pl
from jax.experimental.pallas import tpu as pltpu
from jax.sharding import Mesh
from jax.sharding import PartitionSpec as P

HDIM = 64
HALF = 32
FF = 8192
STEP = 10
Z, X, YH, YL, C = "seq_0", "seq_1", "seq_2", "ffn_0", "ffn_1"
FFN = (YL, C)
SEQ = (Z, X, YH)
SEQ_FFN = (Z, X, YH, YL, C)
ZX = (Z, X)
YY = (YH, YL)
EIGHT = (YH, YL, C)
TILE = 256

norm_eps = 1e-05
rope_base = 10000.0
xpos_base = 512.0
clip_limit = 1.0
beta_first = 0.9
beta_second = 0.95
adam_eps = 1e-08
decay_rate = 0.1
matrix_rate = 0.04
norm_rate = 0.6

F32 = jnp.float32
BF16 = jnp.bfloat16
SWAP = [(0, 1), (1, 0)]


def xor_pairs(count, k):
    return [(i, i ^ k) for i in range(count)]


def dot(a, b, da, db):
    return lax.dot_general(a, b, (((da,), (db,)), ((), ())), preferred_element_type=F32)


def eight_parts(own):
    lines = [own] + [lax.ppermute(own, YY, xor_pairs(4, k)) for k in (1, 2, 3)]
    parts = []
    for line in lines:
        parts += [line, lax.ppermute(line, C, SWAP)]
    return parts


def eight_gather(own):
    return jnp.concatenate(eight_parts(own), axis=0)


def eight_scatter(partial):
    tokens, width = partial.shape
    share = tokens // 8
    low = partial.astype(BF16).reshape(4, 2, share, width)
    got = lax.ppermute(low[:, 1], C, SWAP)
    both = partial.reshape(4, 2, share, width)[:, 0] + got.astype(F32)
    total = both[0]
    sent = both.astype(BF16)
    for k in (1, 2, 3):
        total = total + lax.ppermute(sent[k], YY, xor_pairs(4, k)).astype(F32)
    return total


def copies_of(shard, axis):
    copies = jnp.broadcast_to(shard, (lax.axis_size(axis), *shard.shape))
    return lax.all_to_all(copies, axis, split_axis=0, concat_axis=0, tiled=True)


def share_order(sums):
    shares = sums.reshape(sums.shape[0], 2, 2, 2, -1)
    for axis, name in ((1, YH), (2, YL), (3, C)):
        shares = jnp.where(lax.axis_index(name) == 0, shares, jnp.flip(shares, axis))
    return shares.reshape(sums.shape)


def eight_sum(sums):
    return share_order(jnp.sum(copies_of(share_order(sums), EIGHT), axis=0))


def turned(tile):
    return jnp.transpose(tile.astype(F32)).astype(BF16)


def forward_kernel(qkv_ref, start_ref, out_ref, top_ref, q_s, k_s, v_s, s_s):
    blocks = q_s.shape[0]
    pieces = TILE // 128
    for i in range(blocks):
        for j in range(pieces):
            part = slice(j * 128, (j + 1) * 128)
            q_s[i, :, part] = qkv_ref[i * pieces + j, 0]
            k_s[i, part, :] = turned(qkv_ref[i * pieces + j, 1])
            v_s[i, :, part] = qkv_ref[i * pieces + j, 2]
    factor = math.log2(math.e) / math.sqrt(HDIM)
    key_line = lax.broadcasted_iota(jnp.int32, (TILE, TILE), 0)
    query_line = lax.broadcasted_iota(jnp.int32, (TILE, TILE), 1)
    for i in range(blocks):
        query = q_s[i]
        begin = start_ref[:, i * TILE : (i + 1) * TILE]
        peak = None
        for b in range(i + 1):
            s = dot(k_s[b], query, 1, 0) * factor
            keep = key_line >= begin - b * TILE
            if b == i:
                keep = keep & (key_line <= query_line)
            s = jnp.where(keep, s, -1e30)
            s_s[b] = s
            high = jnp.max(s, axis=0, keepdims=True)
            peak = high if peak is None else jnp.maximum(peak, high)
        total = jnp.zeros((1, TILE), F32)
        acc = jnp.zeros((HDIM, TILE), F32)
        for b in range(i + 1):
            e = jnp.exp2(s_s[b] - peak)
            total = total + jnp.sum(e, axis=0, keepdims=True)
            acc = acc + dot(v_s[b], e.astype(BF16), 1, 0)
        out = acc / total
        for j in range(pieces):
            out_ref[i * pieces + j] = out[:, j * 128 : (j + 1) * 128]
        top_ref[:, i * TILE : (i + 1) * TILE] = peak + jnp.log2(total)


def backward_kernel(
    qkv_ref, do_ref, o_ref, top_ref, start_ref, rot_ref, out_ref,
    qt_s, kt_s, dot_s, q_s, k_s, v_s, do_s, dq_s, dk_s, dv_s,
):
    blocks = qt_s.shape[0]
    pieces = TILE // 128
    for i in range(blocks):
        for j in range(pieces):
            part = slice(j * 128, (j + 1) * 128)
            c = i * pieces + j
            qt_s[i, :, part] = qkv_ref[c, 0]
            kt_s[i, :, part] = qkv_ref[c, 1]
            dot_s[i, :, part] = do_ref[c]
            q_s[i, part, :] = turned(qkv_ref[c, 0])
            k_s[i, part, :] = turned(qkv_ref[c, 1])
            v_s[i, part, :] = turned(qkv_ref[c, 2])
            do_s[i, part, :] = turned(do_ref[c])
    scale = 1.0 / math.sqrt(HDIM)
    factor = math.log2(math.e) * scale
    key_line = lax.broadcasted_iota(jnp.int32, (TILE, TILE), 0)
    query_line = lax.broadcasted_iota(jnp.int32, (TILE, TILE), 1)
    for i in range(blocks):
        span = slice(i * TILE, (i + 1) * TILE)
        begin = start_ref[:, span]
        top = top_ref[:, span]
        delta = jnp.concatenate(
            [
                jnp.sum(
                    do_ref[i * pieces + j].astype(F32) * o_ref[i * pieces + j],
                    axis=0,
                    keepdims=True,
                )
                for j in range(pieces)
            ],
            axis=1,
        )
        dq = jnp.zeros((HDIM, TILE), F32)
        for b in range(i + 1):
            s = dot(k_s[b], qt_s[i], 1, 0) * factor
            keep = key_line >= begin - b * TILE
            if b == i:
                keep = keep & (key_line <= query_line)
            p = jnp.where(keep, jnp.exp2(s - top), 0.0)
            dp = dot(v_s[b], dot_s[i], 1, 0)
            ds = (p * (dp - delta)).astype(BF16)
            dq = dq + dot(kt_s[b], ds, 1, 0)
            dk = dot(ds, q_s[i], 1, 0)
            dv = dot(p.astype(BF16), do_s[i], 1, 0)
            if b == i:
                dk_s[b] = dk
                dv_s[b] = dv
            else:
                dk_s[b] += dk
                dv_s[b] += dv
        dq_s[i] = dq
    for i in range(blocks):
        span = slice(i * TILE, (i + 1) * TILE)
        dq = dq_s[i] * scale
        dk = jnp.transpose(dk_s[i]) * scale
        dv = jnp.transpose(dv_s[i])
        results = []
        for n, g in enumerate((dq, dk)):
            co, si = rot_ref[2 * n, :, span], rot_ref[2 * n + 1, :, span]
            front, back = g[:HALF], g[HALF:]
            results.append(
                jnp.concatenate([front * co + back * si, back * co - front * si], axis=0)
            )
        results.append(dv)
        for n, g in enumerate(results):
            for j in range(pieces):
                out_ref[i * pieces + j, n] = g[:, j * 128 : (j + 1) * 128].astype(BF16)


def attend(qkv, start):
    count = qkv.shape[0]
    blocks = count * 128 // TILE
    return pl.pallas_call(
        forward_kernel,
        out_shape=(
            jax.ShapeDtypeStruct((count, HDIM, 128), F32),
            jax.ShapeDtypeStruct((1, count * 128), F32),
        ),
        scratch_shapes=[
            pltpu.VMEM((blocks, HDIM, TILE), BF16),
            pltpu.VMEM((blocks, TILE, HDIM), BF16),
            pltpu.VMEM((blocks, HDIM, TILE), BF16),
            pltpu.VMEM((blocks, TILE, TILE), F32),
        ],
        compiler_params=pltpu.CompilerParams(vmem_limit_bytes=32 * 1024 * 1024),
        cost_estimate=pl.CostEstimate(
            flops=2000000000, bytes_accessed=4000000, transcendentals=2400000
        ),
        name="attend",
    )(qkv, start)


def attend_back(qkv, d_out, out, top, start, tables):
    count = qkv.shape[0]
    blocks = count * 128 // TILE
    wide = pltpu.VMEM((blocks, HDIM, TILE), BF16)
    tall = pltpu.VMEM((blocks, TILE, HDIM), BF16)
    return pl.pallas_call(
        backward_kernel,
        out_shape=jax.ShapeDtypeStruct((count, 3, HDIM, 128), BF16),
        scratch_shapes=[
            wide, wide, wide, tall, tall, tall, tall,
            pltpu.VMEM((blocks, HDIM, TILE), F32),
            pltpu.VMEM((blocks, TILE, HDIM), F32),
            pltpu.VMEM((blocks, TILE, HDIM), F32),
        ],
        compiler_params=pltpu.CompilerParams(vmem_limit_bytes=40 * 1024 * 1024),
        cost_estimate=pl.CostEstimate(
            flops=6000000000, bytes_accessed=6000000, transcendentals=2400000
        ),
        name="attend_back",
    )(qkv, d_out, out, top, start, tables)


def rotation_tables(row_slots):
    index_half = np.arange(HALF, dtype=np.float64)
    places = np.arange(row_slots, dtype=np.float64) - row_slots // 2
    inverse = rope_base ** (-2.0 * index_half / HDIM)
    angles = inverse[:, None] * places[None, :]
    zeta = (2.0 * index_half + 0.4 * HDIM) / (1.4 * HDIM)
    stretch = zeta[:, None] ** (places[None, :] / xpos_base)
    cosine, sine = np.cos(angles), np.sin(angles)
    tables = [cosine * stretch, sine * stretch, cosine / stretch, sine / stretch]
    return np.stack(tables).astype(np.float32)


def moments(values):
    center = jnp.mean(values, axis=-1, keepdims=True)
    spread = jnp.mean(jnp.square(values - center), axis=-1, keepdims=True)
    inverse = lax.rsqrt(spread + norm_eps)
    return (values - center) * inverse, inverse


def norm_back(upstream, gain, normed, inverse):
    scaled = upstream * gain
    return inverse * (
        scaled
        - jnp.mean(scaled, axis=-1, keepdims=True)
        - normed * jnp.mean(scaled * normed, axis=-1, keepdims=True)
    )


def adam_update(weight, moment, squares, gradient, factor, step_rate, decay_weight):
    clipped = gradient * factor
    moment_new = beta_first * moment + (1.0 - beta_first) * clipped
    squares_new = beta_second * squares + (1.0 - beta_second) * clipped * clipped
    moment_hat = moment_new / (1.0 - beta_first**STEP)
    squares_hat = squares_new / (1.0 - beta_second**STEP)
    updated = weight - step_rate * (
        moment_hat / (jnp.sqrt(squares_hat) + adam_eps) + decay_weight * weight
    )
    return (updated, moment_new, squares_new)


def shards(
    hidden_in, cotangent, doc_lengths,
    inward, inward_moment, inward_squares,
    outward, outward_moment, outward_squares,
    upward, upward_moment, upward_squares,
    downward, downward_moment, downward_squares,
    prenorm, prenorm_moment, prenorm_squares,
    subnorm, subnorm_moment, subnorm_squares,
):
    rows, seq_slots, width = hidden_in.shape
    quarter = cotangent.shape[1]
    group_slots = 2 * seq_slots
    row_slots = group_slots * lax.axis_size(ZX)
    half = inward.shape[2] // 2
    heads = half // HDIM
    tokens = rows * group_slots
    share = rows * quarter
    zx = lax.axis_index(ZX)
    row_index = lax.axis_index(Z)
    yh = lax.axis_index(YH)
    core = lax.axis_index(C)
    ffn = lax.axis_index(FFN)
    me = lax.axis_index(EIGHT)
    low_side = yh == 0

    def mine_theirs(array, axis):
        low = array.astype(BF16)
        mine = lax.dynamic_slice_in_dim(low, yh * half, half, axis)
        theirs = lax.dynamic_slice_in_dim(low, (1 - yh) * half, half, axis)
        return mine, theirs

    def in_order(own, other):
        return jnp.concatenate(
            [jnp.where(low_side, own, other), jnp.where(low_side, other, own)], axis=0
        )

    def gathered(lines):
        other = lax.ppermute(jnp.concatenate([t for _, t in lines], axis=1), YH, SWAP)
        own = jnp.concatenate([m for m, _ in lines], axis=1)
        return lax.all_gather(in_order(own, other), ZX, axis=0, tiled=True)

    def rows_of(pair, order):
        return tuple(jnp.transpose(t, order).reshape(seq_slots, -1) for t in pair)

    in_pair = rows_of(mine_theirs(inward, 2), (0, 1, 2))
    out_pair = rows_of(mine_theirs(outward, 0), (1, 0))
    up_pair = rows_of(mine_theirs(upward, 2), (0, 1, 2))
    down_pair = rows_of(mine_theirs(downward, 1), (2, 0, 1))
    w_in = gathered([in_pair])
    w_rest = gathered([out_pair, up_pair, down_pair])
    hidden_units = 4 * half
    w_out = w_rest[:, :half]
    w_up = w_rest[:, half : half + hidden_units]
    w_down = w_rest[:, half + hidden_units :]

    doc_ends = jnp.cumsum(doc_lengths, axis=1)
    places = jnp.arange(row_slots, dtype=jnp.int32)
    my_ends = lax.dynamic_slice_in_dim(doc_ends, row_index, 1, 0)
    start = jnp.max(
        jnp.where(places[None, :] >= my_ends.reshape(-1, 1), my_ends.reshape(-1, 1), 0),
        axis=0,
        keepdims=True,
    )
    own_places = zx * group_slots + me * quarter + jnp.arange(quarter, dtype=jnp.int32)
    own_usable = (own_places[None, :] < doc_ends[:, -1:]).astype(F32).reshape(share, 1)

    t_rel = jnp.arange(tokens, dtype=jnp.int32)
    rel_share, rel_row, rel_slot = (
        t_rel // share,
        (t_rel % share) // quarter,
        t_rel % quarter,
    )
    rel_place = rel_row * group_slots + (rel_share ^ me) * quarter + rel_slot
    order = (jnp.arange(tokens, dtype=jnp.int32)[:, None] == rel_place[None, :]).astype(BF16)

    half_slots = seq_slots // 2
    sent = lax.dynamic_slice_in_dim(hidden_in, core * half_slots, half_slots, 1)
    got_mine = lax.ppermute(sent, YY, [(i, 3 - i) for i in range(4)])
    got_other = lax.ppermute(got_mine, C, SWAP)
    first_core = core == 0
    other_half = jnp.concatenate(
        [
            jnp.where(first_core, got_mine, got_other),
            jnp.where(first_core, got_other, got_mine),
        ],
        axis=1,
    )
    hidden = jnp.concatenate(
        [jnp.where(low_side, hidden_in, other_half), jnp.where(low_side, other_half, hidden_in)],
        axis=1,
    ).reshape(tokens, width)
    own_hidden = (
        lax.dynamic_slice_in_dim(hidden_in, ffn * quarter, quarter, 1)
        .astype(F32)
        .reshape(share, width)
    )
    own_cot = cotangent.astype(F32).reshape(share, width)
    df = eight_gather((own_usable * own_cot).astype(BF16))

    normed_one, _ = moments(hidden.astype(F32))
    a = (normed_one * prenorm[0] + prenorm[1]).astype(BF16)
    proj = dot(w_in, a, 0, 1).reshape(3, heads, HDIM, rows, group_slots)
    tables = jnp.asarray(rotation_tables(row_slots))
    near = lax.dynamic_slice_in_dim(tables, zx * group_slots, group_slots, 2)

    def rotate(values, cosine, sine):
        front, back = values[:, :HALF], values[:, HALF:]
        cosine, sine = cosine[None, :, None, :], sine[None, :, None, :]
        return jnp.concatenate(
            [front * cosine - back * sine, front * sine + back * cosine], axis=1
        )

    qkv = jnp.stack(
        [rotate(proj[0], near[0], near[1]), rotate(proj[1], near[2], near[3]), proj[2]]
    ).astype(BF16)
    qkv = jnp.transpose(qkv, (3, 1, 0, 2, 4)).reshape(rows * heads, 3, HDIM, group_slots)
    qkv = lax.all_to_all(qkv, ZX, 0, 0, tiled=True)
    o_head, top = attend(qkv, start)

    def to_tokens(chunks):
        parts = chunks.shape[1]
        back = lax.all_to_all(chunks, ZX, 0, 0, tiled=True)
        back = back.reshape(rows, heads, parts, HDIM, group_slots)
        return jnp.transpose(back, (2, 1, 3, 0, 4)).reshape(parts * heads * HDIM, tokens)

    o_wide = to_tokens(o_head.astype(BF16)[:, None])
    o = dot(order, o_wide, 0, 1)

    sub = lax.dynamic_slice_in_dim(subnorm, yh * half, half, 2)
    gain_o, shift_o = sub[0, 0], sub[1, 0]
    gain_h, shift_h = sub[0, 1:].reshape(-1), sub[1, 1:].reshape(-1)
    sums = eight_sum(jnp.stack([jnp.sum(o, axis=1), jnp.sum(o * o, axis=1)]))
    center = sums[0] / width
    inv_o = lax.rsqrt(sums[1] / width - center * center + norm_eps)[:, None]
    o_hat = (o - center[:, None]) * inv_o
    c = (o_hat * gain_o + shift_o).astype(BF16)
    attn = eight_scatter(dot(c, w_out, 1, 1))
    r1 = own_hidden + own_usable * attn
    r1_hat, r1_inv = moments(r1)
    bb = eight_gather((r1_hat * prenorm[2] + prenorm[3]).astype(BF16))

    dhn = dot(df, w_down, 1, 0)
    u = dot(bb, w_up, 1, 0)
    cdf = 0.5 * (1.0 + lax.erf(u * (1.0 / math.sqrt(2.0))))
    h = u * cdf
    slope = cdf + u * (jnp.exp(-0.5 * u * u) * (1.0 / math.sqrt(2.0 * math.pi)))
    scaled = dhn * gain_h
    sums = eight_sum(
        jnp.stack(
            [
                jnp.sum(h, axis=1),
                jnp.sum(h * h, axis=1),
                jnp.sum(scaled, axis=1),
                jnp.sum(scaled * h, axis=1),
            ]
        )
    )
    center = sums[0] / FF
    inv_h = lax.rsqrt(sums[1] / FF - center * center + norm_eps)
    mean_scaled = sums[2] / FF
    mean_both = inv_h * (sums[3] / FF - center * mean_scaled)
    center, inv_h, mean_scaled, mean_both = (
        t[:, None] for t in (center, inv_h, mean_scaled, mean_both)
    )
    h_hat = (h - center) * inv_h
    hn = (h_hat * gain_h + shift_h).astype(BF16)
    du = (inv_h * (scaled - mean_scaled - h_hat * mean_both) * slope).astype(BF16)
    sub_gain_h = jnp.sum(dhn * h_hat, axis=0)
    sub_shift_h = jnp.sum(dhn, axis=0)
    dbb = eight_scatter(dot(du, w_up, 1, 1))
    f = eight_scatter(dot(hn, w_down, 1, 1))
    hidden_out = (r1 + own_usable * f).astype(BF16).reshape(rows, quarter, width)
    g_mlp = jnp.concatenate([dot(df, hn, 0, 0), dot(bb, du, 0, 0)], axis=1).astype(BF16)
    g_mlp = lax.psum_scatter(g_mlp, ZX, scatter_dimension=0, tiled=True)

    dr1 = own_cot + norm_back(dbb, prenorm[2], r1_hat, r1_inv)
    pre_three = jnp.stack([jnp.sum(dbb * r1_hat, axis=0), jnp.sum(dbb, axis=0)])
    dattn = eight_gather((own_usable * dr1).astype(BF16))

    dc = dot(dattn, w_out, 1, 0)
    sub_gain_o = jnp.sum(dc * o_hat, axis=0)
    sub_shift_o = jnp.sum(dc, axis=0)
    scaled_o = dc * gain_o
    sums = eight_sum(jnp.stack([jnp.sum(scaled_o, axis=1), jnp.sum(scaled_o * o_hat, axis=1)]))
    do = inv_o * (scaled_o - (sums[0] / width)[:, None] - o_hat * (sums[1] / width)[:, None])
    do_wide = dot(do.astype(BF16), order, 0, 1).astype(BF16)
    do_wide = do_wide.reshape(heads, HDIM, rows, group_slots)
    do_head = jnp.transpose(do_wide, (2, 0, 1, 3)).reshape(rows * heads, HDIM, group_slots)
    do_head = lax.all_to_all(do_head, ZX, 0, 0, tiled=True)
    dqkv = attend_back(qkv, do_head, o_head, top, start, tables)
    dproj = to_tokens(dqkv)

    g_att = jnp.concatenate([dot(a, dproj, 0, 1), dot(dattn, c, 0, 0)], axis=1).astype(BF16)
    g_att = lax.psum_scatter(g_att, ZX, scatter_dimension=0, tiled=True)
    dproj_rel = dot(order, dproj, 0, 1).astype(BF16)
    da = eight_scatter(dot(dproj_rel, w_in, 1, 1))
    x_hat, x_inv = moments(own_hidden)
    own_grad = dr1 + norm_back(da, prenorm[0], x_hat, x_inv)
    pre_one = jnp.stack([jnp.sum(da * x_hat, axis=0), jnp.sum(da, axis=0)])
    own_grad = own_grad.astype(BF16).reshape(rows, quarter, width)
    core_grad = lax.ppermute(own_grad, C, SWAP)
    pair = jnp.concatenate(
        [jnp.where(first_core, own_grad, core_grad), jnp.where(first_core, core_grad, own_grad)],
        axis=1,
    )
    line_grad = lax.ppermute(pair, YL, SWAP)
    first_line = lax.axis_index(YL) == 0
    input_grad = jnp.concatenate(
        [jnp.where(first_line, pair, line_grad), jnp.where(first_line, line_grad, pair)], axis=1
    )

    g_mlp = g_mlp.astype(F32)
    g_att = g_att.astype(F32)
    local = jnp.sum(g_mlp * g_mlp) + jnp.sum(g_att * g_att)
    sub_grad = jnp.stack(
        [
            jnp.concatenate([sub_gain_o, sub_gain_h]),
            jnp.concatenate([sub_shift_o, sub_shift_h]),
        ]
    )
    pre_grad = jnp.concatenate([pre_one, pre_three], axis=0)

    def parted(value):
        high = value.astype(BF16)
        return jnp.stack([high, (value - high.astype(F32)).astype(BF16)])

    small = jnp.concatenate(
        [pre_grad.astype(BF16).ravel(), sub_grad.astype(BF16).ravel(), parted(local)]
    )
    pre_size, sub_size = pre_grad.size, sub_grad.size
    total = jnp.sum(copies_of(small, ZX).astype(F32), axis=0)
    sub_total = total[pre_size : pre_size + sub_size]
    local = total[pre_size + sub_size] + total[pre_size + sub_size + 1]
    local = local + jnp.sum(sub_total * sub_total)
    small = jnp.concatenate([total[:pre_size].astype(BF16), parted(local)])
    total = jnp.sum(copies_of(small, EIGHT).astype(F32), axis=0)
    pre_total = total[:pre_size].reshape(pre_grad.shape)
    squares_total = total[pre_size] + total[pre_size + 1] + jnp.sum(pre_total * pre_total)
    grad_norm = jnp.sqrt(squares_total)
    factor = jnp.minimum(1.0, clip_limit / (grad_norm + 1e-06))

    own_sub = sub_total.reshape(2, 5, half).astype(BF16)
    their_sub = lax.ppermute(own_sub, YH, SWAP)
    sub_full = jnp.concatenate(
        [jnp.where(low_side, own_sub, their_sub), jnp.where(low_side, their_sub, own_sub)], axis=2
    ).astype(F32)
    grads = jnp.concatenate([g_att, g_mlp], axis=1).astype(BF16)
    keep = lax.dynamic_slice_in_dim(grads, yh * seq_slots, seq_slots, 0)
    give = lax.dynamic_slice_in_dim(grads, (1 - yh) * seq_slots, seq_slots, 0)
    take = lax.ppermute(give, YH, SWAP)

    def whole(begin, count):
        mine = keep[:, begin : begin + count * half].reshape(seq_slots, count, half)
        theirs = take[:, begin : begin + count * half].reshape(seq_slots, count, half)
        return jnp.concatenate(
            [jnp.where(low_side, mine, theirs), jnp.where(low_side, theirs, mine)], axis=2
        ).astype(F32)

    grad_in = whole(0, 3)
    grad_out = whole(3 * half, 1)[:, 0].T
    grad_down = jnp.transpose(whole(4 * half, 4), (1, 2, 0))
    grad_up = whole(8 * half, 4)

    new_in = adam_update(
        inward, inward_moment, inward_squares, grad_in, factor, matrix_rate, decay_rate
    )
    new_out = adam_update(
        outward, outward_moment, outward_squares, grad_out, factor, matrix_rate, decay_rate
    )
    new_up = adam_update(
        upward, upward_moment, upward_squares, grad_up, factor, matrix_rate, decay_rate
    )
    new_down = adam_update(
        downward, downward_moment, downward_squares, grad_down, factor, matrix_rate, decay_rate
    )
    new_pre = adam_update(
        prenorm, prenorm_moment, prenorm_squares, pre_total, factor, norm_rate, 0.0
    )
    new_sub = adam_update(
        subnorm, subnorm_moment, subnorm_squares, sub_full, factor, norm_rate, 0.0
    )
    return (
        hidden_out, input_grad, *new_in, *new_out, *new_up, *new_down, *new_pre, *new_sub, grad_norm,
    )


def solution(mesh):
    finer = Mesh(mesh.devices.reshape(4, 4, 2, 2, 2), SEQ_FFN)
    matrices = (P(SEQ, None, FFN),) * 3 + (P(FFN, SEQ),) * 3
    matrices += (P(SEQ, None, FFN),) * 3 + (P(None, FFN, SEQ),) * 3
    norms = (P(),) * 3 + (P(None, None, FFN),) * 3
    return jax.shard_map(
        shards,
        mesh=finer,
        in_specs=(P(None, SEQ, None), P(None, SEQ_FFN, None), P(), *matrices, *norms),
        out_specs=(P(None, SEQ_FFN, None), P(None, SEQ, None), *matrices, *norms, P()),
        check_vma=False,
    )
```

time: 1760 us -> 670 us (0.38)
  waiting for transfers between devices: 906 us -> 235 us
  local copies, waits for them, and re-layouts: 311 us -> 115 us
  matrix products: 185 us -> 55.3 us
  other arithmetic: 174 us -> 87.1 us
    all_gather x3 -> x2, waiting for transfers between devices: 372 us -> 20.1 us  [gathered(): return lax.all_gather(in_order(own, other), ZX, axis=0, tiled=True)]
    reduce_scatter x3 -> x2, waiting for transfers between devices: 359 us -> 76.7 us  [the longest x1 76.7 us: shards(): g_mlp = lax.psum_scatter(g_mlp, ZX, scatter_dimension=0, tiled=True)]
    dot_general x36 -> x14, matrix products: 185 us -> 55.3 us  [dot(): lax.dot_general(a, b, (((da,), (db,)), ((), ())), preferred_element_type=...]
    all_to_all x20 -> x6, waiting for transfers between devices: 174 us -> 47.9 us  [the longest x2 19.1 us: to_tokens(): back = lax.all_to_all(chunks, ZX, 0, 0, tiled=True)]
    ppermute x0 -> x45, waiting for transfers between devices: none -> 90.5 us  [the longest x12 38.9 us: eight_scatter(): total = total + lax.ppermute(sent[k], YY, xor_pairs(4, k)).astype(F32)]
    all_to_all x20 -> x6, starting transfers between devices: 117 us -> 31 us  [the longest x3 18.8 us: copies_of(): return lax.all_to_all(copies, axis, split_axis=0, concat_axis=0, tiled=True)]
    ppermute x0 -> x45, starting transfers between devices: none -> 69.9 us  [the longest x12 20.7 us: eight_parts(): parts += [line, lax.ppermute(line, C, SWAP)]]
    reshape x12 -> x14, local copies, waits for them, and re-layouts: 71 us -> 12.8 us  [the longest x3 4.15 us: share_order(): return shares.reshape(sums.shape)]
  transfers between devices with their start and end apart: 26 -> 55, of which waited for: 23 -> 32; matrix products, arithmetic and copies ran while one was open for 21% -> 18% of each run, Pallas kernels for 0% -> 1%
where the time goes in v1:
time: 670 us; the launch traced here: 660 us
  waiting for transfers between devices  235 us (35%)
  local copies, waits for them, and re-layouts  115 us (17%)
  starting transfers between devices  101 us (15%)
  other arithmetic  87.1 us (13%)
  matrix products  55.3 us (8%)
  blocking collectives  27.6 us (4%)
  between operations  22.3 us (3%)
  Pallas kernels  16.5 us (2%)
    reduce_scatter x1, waiting for transfers between devices, shards(): g_mlp = lax.psum_scatter(g_mlp, ZX, scatter_dimension=0, tiled=True)  76.7 us
    dot_general x14, matrix products, dot(): lax.dot_general(a, b, (((da,), (db,)), ((), ())), preferred_element_type=...  55.3 us
    unnamed x229, local copies, waits for them, and re-layouts  48.4 us
    ppermute x12, waiting for transfers between devices, eight_scatter(): total = total + lax.ppermute(sent[k], YY, xor_pairs(4, k)).astype(F32)  38.9 us
    ppermute x12, starting transfers between devices, eight_parts(): parts += [line, lax.ppermute(line, C, SWAP)]  20.7 us
    all_gather x2, waiting for transfers between devices, gathered(): return lax.all_gather(in_order(own, other), ZX, axis=0, tiled=True)  20.1 us
    all_to_all x2, waiting for transfers between devices, to_tokens(): back = lax.all_to_all(chunks, ZX, 0, 0, tiled=True)  19.1 us
    all_to_all x3, starting transfers between devices, copies_of(): return lax.all_to_all(copies, axis, split_axis=0, concat_axis=0, tiled=True)  18.8 us
  transfers between devices with their start and end apart: 55, of which 32 were waited for; matrix products, arithmetic and copies ran while one was open for 18% of the time, Pallas kernels for 1%

profile of v1, /device:TPU:1, one launch (start us, length us, event | category | flops | bytes accessed | tf_op | source)
XLA Modules:
  0.0 660.1 jit_solution(8980580980056265585)
XLA Ops:
  8.4 3.8 collective-permute-start
  15.5 3.0 collective-permute-start.3
  18.6 5.2 collective-permute-done.3
  27.7 9.3 %collective-permute-done.1 = bf16[4,32,2048]{2,1,0:T(8,128)(2,1)S(1)} collective-permute-done((bf16[4,32,2048]{2,1,0:T(8,128)(2,1)S(1)}, bf16[4,32,2048]{2,1,0:T(8,128)(2,1)S(1)}, u32[]{:S(2)}, u32[]{:S(2)}) %collective-permute-start.1) | collective-permute-done | bytes 524320 | tf_op jit(solution)/shard_map/ppermute | solution.py:367
  37.0 3.6 collective-permute-start.2
  46.4 20.1 %all-gather.3.cloned.1.call-done = bf16[2048,768]{1,0:T(8,128)(2,1)} async-done(((bf16[128,768]{1,0:T(8,128)(2,1)}), bf16[2048,768]{1,0:T(8,128)(2,1)}) %all-gather.3.cloned.1.call-update) | async-done | bytes 3145744 | tf_op jit(solution)/shard_map/all_gather | solution.py:329
  66.5 4.4 fusion.153
  77.6 4.2 all-to-all-start
  82.7 18.6 %all-to-all-done.qkv_ref = bf16[16,3,64,128]{3,2,1,0:T(8,128)(2,1)S(1)} async-done(((bf16[16,3,64,128]{3,2,1,0:T(8,128)(2,1)}), bf16[16,3,64,128]{3,2,1,0:T(8,128)(2,1)S(1)}, u32[]{:S(2)}, u32[]{:S(2)}) %all-to-all-start) | async-done | bytes 786464 | tf_op jit(solution)/shard_map/all_to_all | solution.py:406
  101.3 4.9 attend.1
  106.9 4.2 all-to-all-start.1
  111.7 10.4 %all-to-all-done.1 = bf16[16,1,64,128]{3,2,1,0:T(8,128)(2,1)} async-done(((bf16[16,1,64,128]{3,2,1,0:T(8,128)(2,1)}), bf16[16,1,64,128]{3,2,1,0:T(8,128)(2,1)}, u32[]{:S(2)}, u32[]{:S(2)}) %all-to-all-start.1) | async-done | bytes 262176 | tf_op jit(solution)/shard_map/all_to_all | solution.py:411
  136.4 7.1 %all-to-all-start.2 = ((f32[8,2,512]{2,1,0:T(2,128)}), f32[8,2,512]{2,1,0:T(2,128)}, u32[]{:S(2)}, u32[]{:S(2)}) async-start(f32[8,2,512]{2,1,0:T(2,128)} %broadcast_in_dim.27), calls=%async_computation.2 | async-start | bytes 65536 | tf_op jit(solution)/shard_map/all_to_all | solution.py:77
  144.9 3.5 all-to-all-done.2
  159.8 4.3 fusion.144
  168.5 3.7 fusion.135
  179.4 8.3 %collective-permute-done.7 = bf16[64,2048]{1,0:T(8,128)(2,1)} collective-permute-done((bf16[64,2048]{1,0:T(8,128)(2,1)}, bf16[64,2048]{1,0:T(8,128)(2,1)}, u32[]{:S(2)}, u32[]{:S(2)}) %collective-permute-start.7) | collective-permute-done | bytes 262176 | tf_op jit(solution)/shard_map/ppermute | solution.py:71
  203.4 8.5 %collective-permute-done.16 = bf16[64,2048]{1,0:T(8,128)(2,1)S(1)} collective-permute-done((bf16[64,2048]{1,0:T(8,128)(2,1)S(1)}, bf16[64,2048]{1,0:T(8,128)(2,1)S(1)}, u32[]{:S(2)}, u32[]{:S(2)}) %collective-permute-start.16) | collective-permute-done | bytes 262176 | tf_op jit(solution)/shard_map/ppermute | solution.py:51
  225.1 4.8 multiply_reduce_fusion.2
  247.3 8.6 %all_to_all.47 = f32[8,4,512]{2,1,0:T(4,128)} all-to-all(f32[8,4,512]{2,1,0:T(4,128)S(1)} %broadcast_in_dim.28), channel_id=1, replica_groups=mesh['seq_0'=4,'seq_1'=4,'seq_2'=2,'ffn_0'=2,'ffn_1'=2] {'seq_2','ffn_0'..., dimensions={0} | all-to-all | bytes 131072 | tf_op jit(solution)/shard_map/all_to_all | solution.py:77
  269.7 4.4 multiply_reduce_fusion.1
  274.0 4.9 fusion.145
  280.6 4.7 fusion.146
  293.0 8.6 %collective-permute-done.29 = bf16[64,2048]{1,0:T(8,128)(2,1)S(1)} collective-permute-done((bf16[64,2048]{1,0:T(8,128)(2,1)S(1)}, bf16[64,2048]{1,0:T(8,128)(2,1)S(1)}, u32[]{:S(2)}, u32[]{:S(2)}) %collective-permute-start.29) | collective-permute-done | bytes 262176 | tf_op jit(solution)/shard_map/ppermute | solution.py:71
  302.9 10.0 %collective-permute-done.25 = bf16[64,2048]{1,0:T(8,128)(2,1)S(1)} collective-permute-done((bf16[64,2048]{1,0:T(8,128)(2,1)S(1)}, bf16[64,2048]{1,0:T(8,128)(2,1)S(1)}, u32[]{:S(2)}, u32[]{:S(2)}) %collective-permute-start.25) | collective-permute-done | bytes 262176 | tf_op jit(solution)/shard_map/ppermute | solution.py:71
  321.2 3.7 collective-permute-start.32
  333.4 4.0 fusion.152
  353.4 8.3 %all_to_all.48 = f32[8,2,512]{2,1,0:T(2,128)} all-to-all(f32[8,2,512]{2,1,0:T(2,128)S(1)} %broadcast_in_dim.29), channel_id=1, replica_groups=mesh['seq_0'=4,'seq_1'=4,'seq_2'=2,'ffn_0'=2,'ffn_1'=2] {'seq_2','ffn_0'..., dimensions={0} | all-to-all | bytes 65536 | tf_op jit(solution)/shard_map/all_to_all | solution.py:77
  377.0 10.6 %all_to_all.49.do_ref = bf16[16,64,128]{2,1,0:T(8,128)(2,1)S(1)} all-to-all(bf16[16,64,128]{2,1,0:T(8,128)(2,1)S(1)} %bitcast.303), channel_id=1, replica_groups=mesh['seq_0'=4,'seq_1'=4,'seq_2'=2,'ffn_0'=2,'ffn_1'=2] {'seq_0','seq_1'}, dimensions={0} | all-to-all | bytes 524288 | tf_op jit(solution)/shard_map/all_to_all | solution.py:478
  387.6 11.7 %attend_back.1 = bf16[16,3,64,128]{3,2,1,0:T(8,128)(2,1)} custom-call(bf16[16,3,64,128]{3,2,1,0:T(8,128)(2,1)S(1)} %all-to-all-done.qkv_ref, bf16[16,64,128]{2,1,0:T(8,128)(2,1)S(1)} %all_to_all.49.do_ref, f32[16,64,128]{2,1,0:T(8,128)S(1)} %get-tuple-element.23.o_ref, f32[1,2048]{1,0:T(1,128)S(1)} %get-tuple-element.24.top_ref, s32[1,2048]{1,0:T(1,128)S(1)} %bitcast.294, ...), custom_call_target="tpu_custom_call" | custom-call | flops 6000000000 | bytes 6000000 | tf_op jit(solution)/shard_map/attend_back/pallas_call | solution.py:233
  399.2 3.7 all-to-all-start.6
  403.1 3.0 add_convert_fusion
  406.9 8.6 %all-to-all-done.6 = bf16[16,3,64,128]{3,2,1,0:T(8,128)(2,1)S(1)} async-done(((bf16[16,3,64,128]{3,2,1,0:T(8,128)(2,1)}), bf16[16,3,64,128]{3,2,1,0:T(8,128)(2,1)S(1)}, u32[]{:S(2)}, u32[]{:S(2)}) %all-to-all-start.6) | async-done | bytes 786464 | tf_op jit(solution)/shard_map/all_to_all | solution.py:411
  417.1 3.4 convolution_convert_fusion.2
  423.0 6.4 copy.398
  430.7 6.2 convolution_convert_fusion
  436.9 4.5 convolution_convert_fusion.1
  441.4 8.5 %pad_maximum_fusion = bf16[2048,2048]{0,1:T(8,128)(2,1)} fusion(bf16[2048,1024]{0,1:T(8,128)(2,1)} %convolution_convert_fusion, bf16[2048,1024]{0,1:T(8,128)(2,1)} %convolution_convert_fusion.1), kind=kLoop, calls=%fused_computation | loop fusion | flops 16777216 | bytes 16777216 | tf_op jit(solution)/shard_map/concatenate | solution.py:462
  450.0 12.4 %copy.400 = bf16[2048,2048]{1,0:T(8,128)(2,1)} copy(bf16[2048,2048]{0,1:T(8,128)(2,1)} %pad_maximum_fusion) | data formatting | bytes 16777216
  463.5 6.2 fusion.147
  474.7 3.4 fusion.125
  481.9 10.7 %collective-permute-done.40 = bf16[64,2048]{1,0:T(8,128)(2,1)S(1)} collective-permute-done((bf16[64,2048]{1,0:T(8,128)(2,1)S(1)}, bf16[64,2048]{1,0:T(8,128)(2,1)S(1)}, u32[]{:S(2)}, u32[]{:S(2)}) %collective-permute-start.40) | collective-permute-done | bytes 262176 | tf_op jit(solution)/shard_map/ppermute | solution.py:71
  498.4 12.6 %collective-permute-done.42 = bf16[4,32,2048]{2,1,0:T(8,128)(2,1)S(1)} collective-permute-done((bf16[4,32,2048]{2,1,0:T(8,128)(2,1)S(1)}, bf16[4,32,2048]{2,1,0:T(8,128)(2,1)S(1)}, u32[]{:S(2)}, u32[]{:S(2)}) %collective-permute-start.42) | collective-permute-done | bytes 524320 | tf_op jit(solution)/shard_map/ppermute | solution.py:495
  515.1 76.7 %reduce-scatter.9.cloned.1.call-done = bf16[128,2048]{1,0:T(8,128)(2,1)} async-done(((bf16[2048,2048]{1,0:T(8,128)(2,1)}), bf16[128,2048]{1,0:T(8,128)(2,1)}) %reduce-scatter.9.cloned.1.call-update) | async-done | bytes 524304 | tf_op jit(solution)/shard_map/reduce_scatter | solution.py:463
  600.2 4.7 all-to-all-start.7
  607.9 5.1 all-to-all-done.7
  614.2 3.0 collective-permute-start.44
  622.2 7.0 %all-to-all-start.8 = ((bf16[8,2,4097]{2,1,0:T(2,128)(2,1)}), bf16[8,2,4097]{2,1,0:T(2,128)(2,1)S(1)}, u32[]{:S(2)}, u32[]{:S(2)}) async-start(bf16[8,2,4097]{2,1,0:T(2,128)(2,1)} %reshape.634), calls=%async_computation.8 | async-start | bytes 270336 | tf_op jit(solution)/shard_map/all_to_all | solution.py:77
  (520 shorter events, 240.3 us)
Async XLA Ops:
  7.2 59.3 %all-gather.3.cloned.1.call-start = ((), (), s32[]{:S(2)}) async-start(), calls=%async_computation.11 | async-start | bytes 3342336 | tf_op jit(solution)/shard_map/all_gather | solution.py:329
  8.4 5.8 collective-permute-start
  15.0 144.8 %all-gather.5.cloned.1.call-start = ((), (), s32[]{:S(2)}) async-start(), calls=%async_computation.12 | async-start | bytes 10027008 | tf_op jit(solution)/shard_map/all_gather | solution.py:329
  15.5 8.3 %collective-permute-start.3 = (bf16[64,2304]{1,0:T(8,128)(2,1)S(1)}, bf16[64,2304]{1,0:T(8,128)(2,1)S(1)}, u32[]{:S(2)}, u32[]{:S(2)}) collective-permute-start(bf16[64,2304]{1,0:T(8,128)(2,1)S(1)} %pad_maximum_fusion.9), channel_id=1, source_target_pairs={{0,4},{4,0},{1,5},{5,1},{2,6},{6,2},{3,7},{7,3},{8,12},{12,8},{9,1... | collective-permute-start | bytes 884744 | tf_op jit(solution)/shard_map/ppermute | solution.py:327
  24.8 12.1 %collective-permute-start.1 = (bf16[4,32,2048]{2,1,0:T(8,128)(2,1)S(1)}, bf16[4,32,2048]{2,1,0:T(8,128)(2,1)S(1)}, u32[]{:S(2)}, u32[]{:S(2)}) collective-permute-start(bf16[4,32,2048]{2,1,0:T(8,128)(2,1)S(1)} %constant_dynamic-slice_fusion.7), channel_id=1, source_target_pairs={{0,6},{2,4},{4,2},{6,0},{1,7},{3,5},{5,3},{7,1},{8,14},{10,12},{12... | collective-permute-start | bytes 1572872 | tf_op jit(solution)/shard_map/ppermute | solution.py:367
  37.0 5.1 collective-permute-start.2
  77.6 23.7 %all-to-all-start = ((bf16[16,3,64,128]{3,2,1,0:T(8,128)(2,1)}), bf16[16,3,64,128]{3,2,1,0:T(8,128)(2,1)S(1)}, u32[]{:S(2)}, u32[]{:S(2)}) async-start(bf16[16,3,64,128]{3,2,1,0:T(8,128)(2,1)} %bitcast.298), calls=%async_computation | async-start | bytes 1572864 | tf_op jit(solution)/shard_map/all_to_all | solution.py:406
  106.9 15.2 %all-to-all-start.1 = ((bf16[16,1,64,128]{3,2,1,0:T(8,128)(2,1)}), bf16[16,1,64,128]{3,2,1,0:T(8,128)(2,1)}, u32[]{:S(2)}, u32[]{:S(2)}) async-start(bf16[16,1,64,128]{3,2,1,0:T(8,128)(2,1)} %convert_bitcast_fusion), calls=%async_computation.1 | async-start | bytes 524288 | tf_op jit(solution)/shard_map/all_to_all | solution.py:411
  136.4 12.0 %all-to-all-start.2 = ((f32[8,2,512]{2,1,0:T(2,128)}), f32[8,2,512]{2,1,0:T(2,128)}, u32[]{:S(2)}, u32[]{:S(2)}) async-start(f32[8,2,512]{2,1,0:T(2,128)} %broadcast_in_dim.27), calls=%async_computation.2 | async-start | bytes 65536 | tf_op jit(solution)/shard_map/all_to_all | solution.py:77
  173.0 14.7 %collective-permute-start.7 = (bf16[64,2048]{1,0:T(8,128)(2,1)}, bf16[64,2048]{1,0:T(8,128)(2,1)}, u32[]{:S(2)}, u32[]{:S(2)}) collective-permute-start(bf16[64,2048]{1,0:T(8,128)(2,1)} %get-tuple-element.251), channel_id=1, source_target_pairs={{0,6},{2,4},{4,2},{6,0},{1,7},{3,5},{5,3},{7,1},{8,14},{10,12},{12... | collective-permute-start | bytes 786440 | tf_op jit(solution)/shard_map/ppermute | solution.py:71
  173.9 13.8 %collective-permute-start.6 = (bf16[64,2048]{1,0:T(8,128)(2,1)}, bf16[64,2048]{1,0:T(8,128)(2,1)}, u32[]{:S(2)}, u32[]{:S(2)}) collective-permute-start(bf16[64,2048]{1,0:T(8,128)(2,1)} %get-tuple-element.252), channel_id=1, source_target_pairs={{0,4},{2,6},{4,0},{6,2},{1,5},{3,7},{5,1},{7,3},{8,12},{10,14},{12... | collective-permute-start | bytes 786440 | tf_op jit(solution)/shard_map/ppermute | solution.py:71
  175.1 12.9 %collective-permute-start.5 = (bf16[64,2048]{1,0:T(8,128)(2,1)}, bf16[64,2048]{1,0:T(8,128)(2,1)}, u32[]{:S(2)}, u32[]{:S(2)}) collective-permute-start(bf16[64,2048]{1,0:T(8,128)(2,1)} %get-tuple-element.250), channel_id=1, source_target_pairs={{0,2},{2,0},{4,6},{6,4},{1,3},{3,1},{5,7},{7,5},{8,10},{10,8},{12,... | collective-permute-start | bytes 786440 | tf_op jit(solution)/shard_map/ppermute | solution.py:71
  190.5 8.5 %collective-permute-start.8 = (bf16[64,2048]{1,0:T(8,128)(2,1)S(1)}, bf16[64,2048]{1,0:T(8,128)(2,1)S(1)}, u32[]{:S(2)}, u32[]{:S(2)}) collective-permute-start(bf16[64,2048]{1,0:T(8,128)(2,1)S(1)} %get-tuple-element.221), channel_id=1, source_target_pairs={{0,1},{1,0},{2,3},{3,2},{4,5},{5,4},{6,7},{7,6},{8,9},{9,8},{10,11... | collective-permute-start | bytes 786440 | tf_op jit(solution)/shard_map/ppermute | solution.py:54
  193.5 7.1 %collective-permute-start.9 = (bf16[64,2048]{1,0:T(8,128)(2,1)S(1)}, bf16[64,2048]{1,0:T(8,128)(2,1)S(1)}, u32[]{:S(2)}, u32[]{:S(2)}) collective-permute-start(bf16[64,2048]{1,0:T(8,128)(2,1)S(1)} %get-tuple-element.221), channel_id=1, source_target_pairs={{0,2},{2,0},{4,6},{6,4},{1,3},{3,1},{5,7},{7,5},{8,10},{10,8},{12,... | collective-permute-start | bytes 786440 | tf_op jit(solution)/shard_map/ppermute | solution.py:51
  193.8 21.0 %collective-permute-start.11 = (bf16[64,2048]{1,0:T(8,128)(2,1)S(1)}, bf16[64,2048]{1,0:T(8,128)(2,1)S(1)}, u32[]{:S(2)}, u32[]{:S(2)}) collective-permute-start(bf16[64,2048]{1,0:T(8,128)(2,1)S(1)} %get-tuple-element.221), channel_id=1, source_target_pairs={{0,4},{2,6},{4,0},{6,2},{1,5},{3,7},{5,1},{7,3},{8,12},{10,14},{12... | collective-permute-start | bytes 786440 | tf_op jit(solution)/shard_map/ppermute | solution.py:51
  195.5 19.3 %collective-permute-start.13 = (bf16[64,2048]{1,0:T(8,128)(2,1)S(1)}, bf16[64,2048]{1,0:T(8,128)(2,1)S(1)}, u32[]{:S(2)}, u32[]{:S(2)}) collective-permute-start(bf16[64,2048]{1,0:T(8,128)(2,1)S(1)} %get-tuple-element.221), channel_id=1, source_target_pairs={{0,6},{2,4},{4,2},{6,0},{1,7},{3,5},{5,3},{7,1},{8,14},{10,12},{12... | collective-permute-start | bytes 786440 | tf_op jit(solution)/shard_map/ppermute | solution.py:51
  199.0 12.9 %collective-permute-start.16 = (bf16[64,2048]{1,0:T(8,128)(2,1)S(1)}, bf16[64,2048]{1,0:T(8,128)(2,1)S(1)}, u32[]{:S(2)}, u32[]{:S(2)}) collective-permute-start(bf16[64,2048]{1,0:T(8,128)(2,1)S(1)} %get-tuple-element.311), channel_id=1, source_target_pairs={{0,2},{2,0},{4,6},{6,4},{1,3},{3,1},{5,7},{7,5},{8,10},{10,8},{12,... | collective-permute-start | bytes 786440 | tf_op jit(solution)/shard_map/ppermute | solution.py:51
  200.6 17.5 %collective-permute-start.18 = (bf16[64,2048]{1,0:T(8,128)(2,1)S(1)}, bf16[64,2048]{1,0:T(8,128)(2,1)S(1)}, u32[]{:S(2)}, u32[]{:S(2)}) collective-permute-start(bf16[64,2048]{1,0:T(8,128)(2,1)S(1)} %get-tuple-element.311), channel_id=1, source_target_pairs={{0,4},{2,6},{4,0},{6,2},{1,5},{3,7},{5,1},{7,3},{8,12},{10,14},{12... | collective-permute-start | bytes 786440 | tf_op jit(solution)/shard_map/ppermute | solution.py:51
  201.4 18.7 %collective-permute-start.20 = (bf16[64,2048]{1,0:T(8,128)(2,1)S(1)}, bf16[64,2048]{1,0:T(8,128)(2,1)S(1)}, u32[]{:S(2)}, u32[]{:S(2)}) collective-permute-start(bf16[64,2048]{1,0:T(8,128)(2,1)S(1)} %get-tuple-element.311), channel_id=1, source_target_pairs={{0,6},{2,4},{4,2},{6,0},{1,7},{3,5},{5,3},{7,1},{8,14},{10,12},{12... | collective-permute-start | bytes 786440 | tf_op jit(solution)/shard_map/ppermute | solution.py:51
  211.9 10.5 %collective-permute-start.10 = (bf16[64,2048]{1,0:T(8,128)(2,1)S(1)}, bf16[64,2048]{1,0:T(8,128)(2,1)S(1)}, u32[]{:S(2)}, u32[]{:S(2)}) collective-permute-start(bf16[64,2048]{1,0:T(8,128)(2,1)S(1)} %collective-permute-done.9), channel_id=1, source_target_pairs={{0,1},{1,0},{2,3},{3,2},{4,5},{5,4},{6,7},{7,6},{8,9},{9,8},{10,11... | collective-permute-start | bytes 786440 | tf_op jit(solution)/shard_map/ppermute | solution.py:54
  214.7 10.1 %collective-permute-start.17 = (bf16[64,2048]{1,0:T(8,128)(2,1)S(1)}, bf16[64,2048]{1,0:T(8,128)(2,1)S(1)}, u32[]{:S(2)}, u32[]{:S(2)}) collective-permute-start(bf16[64,2048]{1,0:T(8,128)(2,1)S(1)} %collective-permute-done.16), channel_id=1, source_target_pairs={{0,1},{1,0},{2,3},{3,2},{4,5},{5,4},{6,7},{7,6},{8,9},{9,8},{10,11... | collective-permute-start | bytes 786440 | tf_op jit(solution)/shard_map/ppermute | solution.py:54
  214.8 7.5 %collective-permute-start.12 = (bf16[64,2048]{1,0:T(8,128)(2,1)S(1)}, bf16[64,2048]{1,0:T(8,128)(2,1)S(1)}, u32[]{:S(2)}, u32[]{:S(2)}) collective-permute-start(bf16[64,2048]{1,0:T(8,128)(2,1)S(1)} %collective-permute-done.11), channel_id=1, source_target_pairs={{0,1},{1,0},{2,3},{3,2},{4,5},{5,4},{6,7},{7,6},{8,9},{9,8},{10,11... | collective-permute-start | bytes 786440 | tf_op jit(solution)/shard_map/ppermute | solution.py:54
  220.1 4.8 collective-permute-start.19
  279.1 7.1 %collective-permute-start.26 = (bf16[4,64,2048]{2,1,0:T(8,128)(2,1)S(1)}, bf16[4,64,2048]{2,1,0:T(8,128)(2,1)S(1)}, u32[]{:S(2)}, u32[]{:S(2)}) collective-permute-start(bf16[4,64,2048]{2,1,0:T(8,128)(2,1)S(1)} %slice_bitcast_fusion.5), channel_id=1, source_target_pairs={{0,1},{1,0},{2,3},{3,2},{4,5},{5,4},{6,7},{7,6},{8,9},{9,8},{10,11... | collective-permute-start | bytes 3145736 | tf_op jit(solution)/shard_map/ppermute | solution.py:66
  285.4 4.9 collective-permute-start.22
  286.8 14.8 %collective-permute-start.29 = (bf16[64,2048]{1,0:T(8,128)(2,1)S(1)}, bf16[64,2048]{1,0:T(8,128)(2,1)S(1)}, u32[]{:S(2)}, u32[]{:S(2)}) collective-permute-start(bf16[64,2048]{1,0:T(8,128)(2,1)S(1)} %get-tuple-element.245), channel_id=1, source_target_pairs={{0,6},{2,4},{4,2},{6,0},{1,7},{3,5},{5,3},{7,1},{8,14},{10,12},{12... | collective-permute-start | bytes 786440 | tf_op jit(solution)/shard_map/ppermute | solution.py:71
  287.7 13.9 %collective-permute-start.28 = (bf16[64,2048]{1,0:T(8,128)(2,1)S(1)}, bf16[64,2048]{1,0:T(8,128)(2,1)S(1)}, u32[]{:S(2)}, u32[]{:S(2)}) collective-permute-start(bf16[64,2048]{1,0:T(8,128)(2,1)S(1)} %get-tuple-element.246), channel_id=1, source_target_pairs={{0,4},{2,6},{4,0},{6,2},{1,5},{3,7},{5,1},{7,3},{8,12},{10,14},{12... | collective-permute-start | bytes 786440 | tf_op jit(solution)/shard_map/ppermute | solution.py:71
  288.9 13.0 %collective-permute-start.27 = (bf16[64,2048]{1,0:T(8,128)(2,1)S(1)}, bf16[64,2048]{1,0:T(8,128)(2,1)S(1)}, u32[]{:S(2)}, u32[]{:S(2)}) collective-permute-start(bf16[64,2048]{1,0:T(8,128)(2,1)S(1)} %get-tuple-element.244), channel_id=1, source_target_pairs={{0,2},{2,0},{4,6},{6,4},{1,3},{3,1},{5,7},{7,5},{8,10},{10,8},{12,... | collective-permute-start | bytes 786440 | tf_op jit(solution)/shard_map/ppermute | solution.py:71
  290.9 22.0 %collective-permute-start.25 = (bf16[64,2048]{1,0:T(8,128)(2,1)S(1)}, bf16[64,2048]{1,0:T(8,128)(2,1)S(1)}, u32[]{:S(2)}, u32[]{:S(2)}) collective-permute-start(bf16[64,2048]{1,0:T(8,128)(2,1)S(1)} %get-tuple-element.248), channel_id=1, source_target_pairs={{0,6},{2,4},{4,2},{6,0},{1,7},{3,5},{5,3},{7,1},{8,14},{10,12},{12... | collective-permute-start | bytes 786440 | tf_op jit(solution)/shard_map/ppermute | solution.py:71
  291.8 21.0 %collective-permute-start.24 = (bf16[64,2048]{1,0:T(8,128)(2,1)S(1)}, bf16[64,2048]{1,0:T(8,128)(2,1)S(1)}, u32[]{:S(2)}, u32[]{:S(2)}) collective-permute-start(bf16[64,2048]{1,0:T(8,128)(2,1)S(1)} %get-tuple-element.249), channel_id=1, source_target_pairs={{0,4},{2,6},{4,0},{6,2},{1,5},{3,7},{5,1},{7,3},{8,12},{10,14},{12... | collective-permute-start | bytes 786440 | tf_op jit(solution)/shard_map/ppermute | solution.py:71
  301.6 11.6 %collective-permute-start.23 = (bf16[64,2048]{1,0:T(8,128)(2,1)S(1)}, bf16[64,2048]{1,0:T(8,128)(2,1)S(1)}, u32[]{:S(2)}, u32[]{:S(2)}) collective-permute-start(bf16[64,2048]{1,0:T(8,128)(2,1)S(1)} %get-tuple-element.247), channel_id=1, source_target_pairs={{0,2},{2,0},{4,6},{6,4},{1,3},{3,1},{5,7},{7,5},{8,10},{10,8},{12,... | collective-permute-start | bytes 786440 | tf_op jit(solution)/shard_map/ppermute | solution.py:71
  314.5 6.8 %collective-permute-start.31 = (bf16[64,2048]{1,0:T(8,128)(2,1)S(1)}, bf16[64,2048]{1,0:T(8,128)(2,1)S(1)}, u32[]{:S(2)}, u32[]{:S(2)}) collective-permute-start(bf16[64,2048]{1,0:T(8,128)(2,1)S(1)} %get-tuple-element.213), channel_id=1, source_target_pairs={{0,2},{2,0},{4,6},{6,4},{1,3},{3,1},{5,7},{7,5},{8,10},{10,8},{12,... | collective-permute-start | bytes 786440 | tf_op jit(solution)/shard_map/ppermute | solution.py:51
  314.8 12.7 %collective-permute-start.33 = (bf16[64,2048]{1,0:T(8,128)(2,1)S(1)}, bf16[64,2048]{1,0:T(8,128)(2,1)S(1)}, u32[]{:S(2)}, u32[]{:S(2)}) collective-permute-start(bf16[64,2048]{1,0:T(8,128)(2,1)S(1)} %get-tuple-element.213), channel_id=1, source_target_pairs={{0,4},{2,6},{4,0},{6,2},{1,5},{3,7},{5,1},{7,3},{8,12},{10,14},{12... | collective-permute-start | bytes 786440 | tf_op jit(solution)/shard_map/ppermute | solution.py:51
  316.6 13.4 %collective-permute-start.35 = (bf16[64,2048]{1,0:T(8,128)(2,1)S(1)}, bf16[64,2048]{1,0:T(8,128)(2,1)S(1)}, u32[]{:S(2)}, u32[]{:S(2)}) collective-permute-start(bf16[64,2048]{1,0:T(8,128)(2,1)S(1)} %get-tuple-element.213), channel_id=1, source_target_pairs={{0,6},{2,4},{4,2},{6,0},{1,7},{3,5},{5,3},{7,1},{8,14},{10,12},{12... | collective-permute-start | bytes 786440 | tf_op jit(solution)/shard_map/ppermute | solution.py:51
  318.4 13.8 %collective-permute-start.30 = (bf16[64,2048]{1,0:T(8,128)(2,1)S(1)}, bf16[64,2048]{1,0:T(8,128)(2,1)S(1)}, u32[]{:S(2)}, u32[]{:S(2)}) collective-permute-start(bf16[64,2048]{1,0:T(8,128)(2,1)S(1)} %get-tuple-element.213), channel_id=1, source_target_pairs={{0,1},{1,0},{2,3},{3,2},{4,5},{5,4},{6,7},{7,6},{8,9},{9,8},{10,11... | collective-permute-start | bytes 786440 | tf_op jit(solution)/shard_map/ppermute | solution.py:54
  321.2 11.0 %collective-permute-start.32 = (bf16[64,2048]{1,0:T(8,128)(2,1)S(1)}, bf16[64,2048]{1,0:T(8,128)(2,1)S(1)}, u32[]{:S(2)}, u32[]{:S(2)}) collective-permute-start(bf16[64,2048]{1,0:T(8,128)(2,1)S(1)} %collective-permute-done.31), channel_id=1, source_target_pairs={{0,1},{1,0},{2,3},{3,2},{4,5},{5,4},{6,7},{7,6},{8,9},{9,8},{10,11... | collective-permute-start | bytes 786440 | tf_op jit(solution)/shard_map/ppermute | solution.py:54
  399.2 16.4 %all-to-all-start.6 = ((bf16[16,3,64,128]{3,2,1,0:T(8,128)(2,1)}), bf16[16,3,64,128]{3,2,1,0:T(8,128)(2,1)S(1)}, u32[]{:S(2)}, u32[]{:S(2)}) async-start(bf16[16,3,64,128]{3,2,1,0:T(8,128)(2,1)} %attend_back.1), calls=%async_computation.6 | async-start | bytes 1572864 | tf_op jit(solution)/shard_map/all_to_all | solution.py:411
  403.0 109.3 %reduce-scatter.7.cloned.1.call-start = ((), (), s32[]{:S(2)}) async-start(), calls=%async_computation.13 | async-start | bytes 4456448 | tf_op jit(solution)/shard_map/reduce_scatter | solution.py:483
  429.5 162.3 %reduce-scatter.9.cloned.1.call-start = ((), (), s32[]{:S(2)}) async-start(), calls=%async_computation.14 | async-start | bytes 8912896 | tf_op jit(solution)/shard_map/reduce_scatter | solution.py:463
  469.8 4.9 collective-permute-start.37
  478.2 14.4 %collective-permute-start.40 = (bf16[64,2048]{1,0:T(8,128)(2,1)S(1)}, bf16[64,2048]{1,0:T(8,128)(2,1)S(1)}, u32[]{:S(2)}, u32[]{:S(2)}) collective-permute-start(bf16[64,2048]{1,0:T(8,128)(2,1)S(1)} %get-tuple-element.242), channel_id=1, source_target_pairs={{0,6},{2,4},{4,2},{6,0},{1,7},{3,5},{5,3},{7,1},{8,14},{10,12},{12... | collective-permute-start | bytes 786440 | tf_op jit(solution)/shard_map/ppermute | solution.py:71
  479.2 13.4 %collective-permute-start.39 = (bf16[64,2048]{1,0:T(8,128)(2,1)S(1)}, bf16[64,2048]{1,0:T(8,128)(2,1)S(1)}, u32[]{:S(2)}, u32[]{:S(2)}) collective-permute-start(bf16[64,2048]{1,0:T(8,128)(2,1)S(1)} %get-tuple-element.243), channel_id=1, source_target_pairs={{0,4},{2,6},{4,0},{6,2},{1,5},{3,7},{5,1},{7,3},{8,12},{10,14},{12... | collective-permute-start | bytes 786440 | tf_op jit(solution)/shard_map/ppermute | solution.py:71
  480.4 12.6 %collective-permute-start.38 = (bf16[64,2048]{1,0:T(8,128)(2,1)S(1)}, bf16[64,2048]{1,0:T(8,128)(2,1)S(1)}, u32[]{:S(2)}, u32[]{:S(2)}) collective-permute-start(bf16[64,2048]{1,0:T(8,128)(2,1)S(1)} %get-tuple-element.241), channel_id=1, source_target_pairs={{0,2},{2,0},{4,6},{6,4},{1,3},{3,1},{5,7},{7,5},{8,10},{10,8},{12,... | collective-permute-start | bytes 786440 | tf_op jit(solution)/shard_map/ppermute | solution.py:71
  497.6 13.4 %collective-permute-start.42 = (bf16[4,32,2048]{2,1,0:T(8,128)(2,1)S(1)}, bf16[4,32,2048]{2,1,0:T(8,128)(2,1)S(1)}, u32[]{:S(2)}, u32[]{:S(2)}) collective-permute-start(bf16[4,32,2048]{2,1,0:T(8,128)(2,1)S(1)} %pad_maximum_fusion.7), channel_id=1, source_target_pairs={{0,2},{2,0},{1,3},{3,1},{4,6},{6,4},{5,7},{7,5},{8,10},{10,8},{9,1... | collective-permute-start | bytes 1572872 | tf_op jit(solution)/shard_map/ppermute | solution.py:495
  600.2 12.8 %all-to-all-start.7 = ((bf16[16,2,5377]{2,1,0:T(2,128)(2,1)}), bf16[16,2,5377]{2,1,0:T(2,128)(2,1)S(1)}, u32[]{:S(2)}, u32[]{:S(2)}) async-start(bf16[16,2,5377]{2,1,0:T(2,128)(2,1)} %reshape.632), calls=%async_computation.7 | async-start | bytes 704512 | tf_op jit(solution)/shard_map/all_to_all | solution.py:77
  605.0 24.2 %collective-permute-start.43 = (bf16[64,3072]{1,0:T(8,128)(2,1)S(1)}, bf16[64,3072]{1,0:T(8,128)(2,1)}, u32[]{:S(2)}, u32[]{:S(2)}) collective-permute-start(bf16[64,3072]{1,0:T(8,128)(2,1)S(1)} %constant_dynamic-slice_fusion.3), channel_id=1, source_target_pairs={{0,4},{4,0},{1,5},{5,1},{2,6},{6,2},{3,7},{7,3},{8,12},{12,8},{9,1... | collective-permute-start | bytes 1179656 | tf_op jit(solution)/shard_map/ppermute | solution.py:539
  614.2 15.0 %collective-permute-start.44 = (bf16[2,5,256]{2,1,0:T(8,128)(2,1)S(1)}, bf16[2,5,256]{2,1,0:T(8,128)(2,1)S(1)}, u32[]{:S(2)}, u32[]{:S(2)}) collective-permute-start(bf16[2,5,256]{2,1,0:T(8,128)(2,1)S(1)} %convert_element_type.303), channel_id=1, source_target_pairs={{0,4},{4,0},{1,5},{5,1},{2,6},{6,2},{3,7},{7,3},{8,12},{12,8},{9,1... | collective-permute-start | bytes 15368 | tf_op jit(solution)/shard_map/ppermute | solution.py:532
  622.2 12.3 %all-to-all-start.8 = ((bf16[8,2,4097]{2,1,0:T(2,128)(2,1)}), bf16[8,2,4097]{2,1,0:T(2,128)(2,1)S(1)}, u32[]{:S(2)}, u32[]{:S(2)}) async-start(bf16[8,2,4097]{2,1,0:T(2,128)(2,1)} %reshape.634), calls=%async_computation.8 | async-start | bytes 270336 | tf_op jit(solution)/shard_map/all_to_all | solution.py:77
  (98 other events, 719.2 us)
Sparse Core Ops, SparseCore 0:
  15.1 51.3 all-gather.2
  68.6 85.2 all-gather.4
  429.6 73.8 reduce-scatter.6
  507.1 84.5 reduce-scatter.8
